TPU v7x, 32 devices: a whole 2x2x4 slice. The times are simulated.
32 devices in a mesh: groups: 2 (over x), gx: 16 (over z, y, core).
Axes of the slice: x: 2, y: 2, z: 4, core: 2. Of those that a mesh axis runs over, the one named last changes fastest.
Arguments:
- counts: int32 [32], P('groups'), parts along dimension 0, may hold values from 4 to 12, as said below
- resid: float32 [3, 512, 1024], P(None, ('groups', 'gx')), parts along dimension 1, may hold values from -6 to 6
- accum: float32 [9, 512, 1024], P(None, ('groups', 'gx')), parts along dimension 1
- mobility: float32 [9, 512, 1024], P(None, ('groups', 'gx')), parts along dimension 1
- trans: float32 [3, 512, 1024], P(None, ('groups', 'gx')), parts along dimension 1, may hold values from 0.02 to 1
- decouple: float32 [2, 512, 1024], P(None, ('groups', 'gx')), parts along dimension 1, may hold values from 0.3 to 1
Outputs:
- correction: float32 [3, 512, 1024], P(None, ('groups', 'gx')), parts along dimension 1
There are 2 independent parts, one for each index of `groups`. A program takes and returns all parts, laid end to end along the dimension named above; each array names one. Nothing has to cross between parts.
Inputs may be any that keep to these rules, and one draw needn't show every extreme that they name: Partition p holds the planes from s_p = counts[0] + ... + counts[p-1] on; s_p - p * 8 lies between -(2) and 2, both ends taken at two neighbouring partitions in every draw, and the counts sum to 128.
All inputs are finite; a program needn't handle non-finite values.
Results may differ from a plain program's by a relative error of at most 0.0003.
Values sent between devices are 32-bit elements; how exact they have to be, the bound alone decides.
A program may use at most 64 MiB of HBM per device.

v0:
```python
import jax
import jax.numpy as jnp
from jax import lax
from jax.sharding import PartitionSpec as P

CX = 8
NY = 32
NZ = 32
CHEB = 6
SWEEPS = 6
CAP = 16


CHEB_LOW = 0.1
CHEB_HIGH = 2.0


def from_behind(block, axis, distance):
    devices = range(lax.axis_size(axis))
    route = [(i - distance, i) for i in devices if i - distance in devices]
    return lax.ppermute(block, axis, route)


def with_halo(value, sides, width):
    for axis, dim in sides:
        size, length = (lax.axis_size(axis), value.shape[dim])
        up = [(i, (i + 1) % size) for i in range(size - 1)]
        down = [(j, i) for i, j in up]
        last = lax.slice_in_dim(value, length - width, length, axis=dim)
        first = lax.slice_in_dim(value, 0, width, axis=dim)
        before = lax.ppermute(last, axis, up)
        after = lax.ppermute(first, axis, down)
        value = jnp.concatenate([before, value, after], axis=dim)
    return value


def plane_next(values):
    return jnp.concatenate([values[..., 1:, :], jnp.zeros_like(values[..., :1, :])], axis=-2)


def plane_prev(values):
    return jnp.concatenate([jnp.zeros_like(values[..., :1, :]), values[..., :-1, :]], axis=-2)


def lane_next(values, stride):
    return jnp.concatenate([values[..., stride:], jnp.zeros_like(values[..., :stride])], axis=-1)


def lane_prev(values, stride):
    return jnp.concatenate([jnp.zeros_like(values[..., :stride]), values[..., :-stride]], axis=-1)


def block_mul(blocks, vector):
    return jnp.stack(
        [
            blocks[3 * row_id] * vector[0]
            + blocks[3 * row_id + 1] * vector[1]
            + blocks[3 * row_id + 2] * vector[2]
            for row_id in range(3)
        ]
    )


def face_sum(trans_plane, trans_row, trans_lane):
    return (
        trans_plane
        + plane_prev(trans_plane)
        + trans_row
        + lane_prev(trans_row, NZ)
        + trans_lane
        + lane_prev(trans_lane, 1)
    )


def fine_apply(vector, accum, mobility, trans_plane, trans_row, trans_lane):
    carried = block_mul(mobility, vector)
    across = trans_plane * plane_next(carried) + plane_prev(trans_plane * carried)
    across = across + trans_row * lane_next(carried, NZ) + lane_prev(trans_row * carried, NZ)
    across = across + trans_lane * lane_next(carried, 1) + lane_prev(trans_lane * carried, 1)
    return (
        block_mul(accum, vector) + face_sum(trans_plane, trans_row, trans_lane) * carried - across
    )


def block_inverse(accum, mobility, trans_plane, trans_row, trans_lane, keep_mask):
    totals = face_sum(trans_plane, trans_row, trans_lane)
    entries = [accum[entry_id] + totals * mobility[entry_id] for entry_id in range(9)]
    cofactor = [
        entries[4] * entries[8] - entries[5] * entries[7],
        entries[2] * entries[7] - entries[1] * entries[8],
        entries[1] * entries[5] - entries[2] * entries[4],
        entries[5] * entries[6] - entries[3] * entries[8],
        entries[0] * entries[8] - entries[2] * entries[6],
        entries[2] * entries[3] - entries[0] * entries[5],
        entries[3] * entries[7] - entries[4] * entries[6],
        entries[1] * entries[6] - entries[0] * entries[7],
        entries[0] * entries[4] - entries[1] * entries[3],
    ]
    determinant = entries[0] * cofactor[0] + entries[1] * cofactor[3] + entries[2] * cofactor[6]
    determinant = jnp.where(keep_mask, determinant, 1.0)
    return jnp.stack([value / determinant for value in cofactor])


def pressure_coefficients(mobile, storage, trans_plane, trans_row, trans_lane):
    coef_plane = trans_plane * (mobile + plane_next(mobile)) * 0.5
    coef_row = trans_row * (mobile + lane_next(mobile, NZ)) * 0.5
    coef_lane = trans_lane * (mobile + lane_next(mobile, 1)) * 0.5
    pivots = (
        storage
        + coef_plane
        + plane_prev(coef_plane)
        + coef_row
        + lane_prev(coef_row, NZ)
        + coef_lane
        + lane_prev(coef_lane, 1)
    )
    return (coef_plane, coef_row, coef_lane, pivots)


def pressure_apply(vector, coeffs):
    coef_plane, coef_row, coef_lane, pivots = coeffs
    across = coef_plane * plane_next(vector) + plane_prev(coef_plane * vector)
    across = across + coef_row * lane_next(vector, NZ) + lane_prev(coef_row * vector, NZ)
    across = across + coef_lane * lane_next(vector, 1) + lane_prev(coef_lane * vector, 1)
    return pivots * vector - across


def shift_pair(upward, downward):
    from_below = from_behind(upward, "gx", 1)
    from_above = from_behind(downward, "gx", -1)
    return (from_below, from_above)


def ragged_halo(values, plane_count, depth):
    upper_edge = lax.dynamic_slice_in_dim(values, plane_count - depth, depth, 1)
    lower_edge = values[:, :depth]
    from_below, from_above = shift_pair(upper_edge, lower_edge)
    extended = jnp.zeros((values.shape[0], values.shape[1] + 6, values.shape[2]), values.dtype)
    extended = extended.at[:, 3 - depth : 3].set(from_below)
    extended = extended.at[:, 3 : 3 + values.shape[1]].set(values)
    return lax.dynamic_update_slice_in_dim(extended, from_above, 3 + plane_count, 1)


def face_halo(values):
    return with_halo(values, (("gx", 1),), 1)


def on_device(counts, resid, accum, mobility, trans, decouple):
    devices_x = lax.axis_size("gx")
    position = lax.axis_index("gx")
    grid_planes = CX * devices_x
    rim_planes = CX // 2 - 2
    starts = jnp.cumsum(counts) - counts
    first_plane = starts[position]
    plane_count = counts[position]
    slot_ids = jnp.arange(CAP)
    owned = slot_ids < plane_count
    global_ids = first_plane + slot_ids
    lane_ids = jnp.arange(NY * NZ)
    keep_rows = lane_ids // NZ < NY - 1
    keep_lanes = lane_ids % NZ < NZ - 1
    keep_planes = owned & (global_ids < grid_planes - 1)
    owned_rows = owned[None, :, None]
    resid_own = jnp.where(owned_rows, resid, 0.0)
    accum_own = jnp.where(owned_rows, accum, 0.0)
    mobility_own = jnp.where(owned_rows, mobility, 0.0)
    trans_plane = jnp.where(keep_planes[:, None], trans[0], 0.0)
    trans_row = jnp.where(owned[:, None] & keep_rows[None, :], trans[1], 0.0)
    trans_lane = jnp.where(owned[:, None] & keep_lanes[None, :], trans[2], 0.0)
    weight_one = decouple[0]
    weight_two = decouple[1]
    source = resid_own[0] + weight_one * resid_own[1] + weight_two * resid_own[2]
    mobile = mobility_own[0] + weight_one * mobility_own[3] + weight_two * mobility_own[6]
    storage = accum_own[0] + weight_one * accum_own[3] + weight_two * accum_own[6]
    fine_stack = jnp.concatenate(
        [accum_own, mobility_own, trans_plane[None], trans_row[None], trans_lane[None], resid_own],
        axis=0,
    )
    fine_ext = ragged_halo(fine_stack, plane_count, 3)
    ext_ids = jnp.arange(CAP + 6)
    ext_global = first_plane - 3 + ext_ids
    inside = (
        (ext_ids >= 1)
        & (ext_ids < plane_count + 5)
        & (ext_global >= 0)
        & (ext_global < grid_planes)
    )
    owned_ext = (ext_ids >= 3) & (ext_ids < plane_count + 3)
    middle = 0.5 * (CHEB_HIGH + CHEB_LOW)
    radius = 0.5 * (CHEB_HIGH - CHEB_LOW)
    aspect = middle / radius
    factor = 1.0 / aspect
    packed = jnp.stack([source, mobile, storage, trans_plane, trans_row, trans_lane])

    def gather_planes(plane_list):
        local_ids = plane_list - first_plane
        usable = (local_ids >= 0) & (local_ids < plane_count)
        picked = jnp.take(packed, jnp.clip(local_ids, 0, CAP - 1), axis=1)
        return jnp.where(usable[None, :, None], picked, 0.0)

    brick_local = gather_planes(position * CX + jnp.arange(CX))
    rim_ids = jnp.arange(rim_planes)
    bottom, top = shift_pair(
        gather_planes((position + 1) * CX + rim_ids),
        gather_planes(position * CX - rim_planes + rim_ids),
    )
    brick = brick_local.at[:, :rim_planes].add(bottom).at[:, CX - rim_planes :].add(top)
    solution = jnp.zeros((CX, NY * NZ), jnp.float32)
    remain = brick[0]
    coef_ext = face_halo(brick[1:6])
    coeffs = pressure_coefficients(coef_ext[0], coef_ext[1], coef_ext[2], coef_ext[3], coef_ext[4])
    inverse = 1.0 / coeffs[3][1 : CX + 1]
    direction = inverse * remain / middle
    for iteration in range(CHEB):
        applied = pressure_apply(face_halo(direction[None])[0], coeffs)[1 : CX + 1]
        solution = solution + direction
        remain = remain - applied
        factor_next = 1.0 / (2.0 * aspect - factor)
        direction = factor_next * factor * direction + 2.0 * factor_next / radius * inverse * remain
        factor = factor_next
    plane_brick = global_ids // CX
    plane_within = global_ids - plane_brick * CX
    own_value = jnp.take(solution, jnp.clip(plane_within, 0, CX - 1), axis=0)
    below_top, above_bottom = shift_pair(
        solution[None, CX - rim_planes :], solution[None, :rim_planes]
    )
    from_lower = jnp.take(
        below_top[0], jnp.clip(plane_within - (CX - rim_planes), 0, rim_planes - 1), axis=0
    )
    from_upper = jnp.take(above_bottom[0], jnp.clip(plane_within, 0, rim_planes - 1), axis=0)
    remote = jnp.where((plane_brick < position)[:, None], from_lower, from_upper)
    part_pressure = jnp.where(
        owned[:, None], jnp.where((plane_brick == position)[:, None], own_value, remote), 0.0
    )
    sub_accum = fine_ext[0:9]
    sub_mobility = fine_ext[9:18]
    sub_plane = fine_ext[18]
    sub_row = fine_ext[19]
    sub_lane = fine_ext[20]
    sub_resid = fine_ext[21:24]
    pressure_ext = ragged_halo(part_pressure[None], plane_count, 1)[0]
    blank = jnp.zeros_like(pressure_ext)
    lifted = jnp.stack([pressure_ext, blank, blank])
    own_target = jnp.where(
        owned_ext[:, None],
        sub_resid - fine_apply(lifted, sub_accum, sub_mobility, sub_plane, sub_row, sub_lane),
        0.0,
    )
    target = jnp.where(
        inside[:, None], ragged_halo(own_target[:, 3 : 3 + CAP], plane_count, 2), 0.0
    )
    inverse_blocks = block_inverse(
        sub_accum, sub_mobility, sub_plane, sub_row, sub_lane, inside[:, None]
    )
    local = jnp.zeros_like(target)
    for sweep_id in range(SWEEPS):
        defect = target - fine_apply(local, sub_accum, sub_mobility, sub_plane, sub_row, sub_lane)
        local = jnp.where(inside[:, None], local + block_mul(inverse_blocks, defect), 0.0)
    return jnp.where(owned_ext[:, None], lifted + local, 0.0)[:, 3 : 3 + CAP]


def solution(mesh):
    in_specs = (
        P("groups"),
        P(None, ("groups", "gx"), None),
        P(None, ("groups", "gx"), None),
        P(None, ("groups", "gx"), None),
        P(None, ("groups", "gx"), None),
        P(None, ("groups", "gx"), None),
    )
    out_specs = P(None, ("groups", "gx"), None)
    return jax.shard_map(
        on_device, mesh=mesh, in_specs=in_specs, out_specs=out_specs, check_vma=False
    )
```

profile of v0, /device:TPU:5, one launch (start us, length us, event | category | flops | bytes accessed | tf_op | source)
XLA Modules:
  0.0 134.1 jit_solution(12631017921376729568)
XLA Ops:
  0.0 1.3 dynamic_slice.15
  1.4 0.7 copy.60
  2.3 0.7 sub.187
  2.9 0.6 dynamic_slice.16
  3.5 1.3 compare_and_fusion.7
  4.8 1.3 compare_and_fusion.2
  6.1 1.3 constant_dynamic-update-slice_fusion.2
  7.4 1.3 constant_dynamic-update-slice_fusion.1
  10.2 2.6 %collective-permute-start.1 = (f32[6,2,1024]{2,1,0:T(2,128)S(1)}, f32[6,2,1024]{2,1,0:T(2,128)S(1)}, u32[]{:S(2)}, u32[]{:S(2)}) collective-permute-start(f32[6,2,1024]{2,1,0:T(2,128)S(1)} %bitcast_select_fusion), channel_id=1, source_target_pairs={{1,0},{2,1},{3,2},{4,3},{5,4},{6,5},{7,6},{8,7},{9,8},{10,9},{11,1... | collective-permute-start | bytes 147464 | tf_op jit(solution)/shard_map/ppermute | solution.py:21
  12.8 1.3 compare_and_fusion.3
  14.8 3.9 %collective-permute-start = (f32[6,2,1024]{2,1,0:T(2,128)S(1)}, f32[6,2,1024]{2,1,0:T(2,128)S(1)}, u32[]{:S(2)}, u32[]{:S(2)}) collective-permute-start(f32[6,2,1024]{2,1,0:T(2,128)S(1)} %bitcast_select_fusion.1), channel_id=1, source_target_pairs={{0,1},{1,2},{2,3},{3,4},{4,5},{5,6},{6,7},{7,8},{8,9},{9,10},{10,1... | collective-permute-start | bytes 147464 | tf_op jit(solution)/shard_map/ppermute | solution.py:21
  19.9 1.0 fusion.109
  20.9 1.9 %collective-permute-start.19 = (f32[24,3,1024]{2,1,0:T(4,128)S(1)}, f32[24,3,1024]{2,1,0:T(4,128)S(1)}, u32[]{:S(2)}, u32[]{:S(2)}) collective-permute-start(f32[24,3,1024]{2,1,0:T(4,128)S(1)} %get-tuple-element.192), channel_id=1, source_target_pairs={{1,0},{2,1},{3,2},{4,3},{5,4},{6,5},{7,6},{8,7},{9,8},{10,9},{11,1... | collective-permute-start | bytes 884744 | tf_op jit(solution)/shard_map/ppermute | solution.py:21
  22.8 4.5 %collective-permute-start.18 = (f32[24,3,1024]{2,1,0:T(4,128)}, f32[24,3,1024]{2,1,0:T(4,128)}, u32[]{:S(2)}, u32[]{:S(2)}) collective-permute-start(f32[24,3,1024]{2,1,0:T(4,128)} %get-tuple-element.193), channel_id=1, source_target_pairs={{0,1},{1,2},{2,3},{3,4},{4,5},{5,6},{6,7},{7,8},{8,9},{9,10},{10,1... | collective-permute-start | bytes 884744 | tf_op jit(solution)/shard_map/ppermute | solution.py:21
  27.4 0.7 compare_select_fusion
  28.0 0.7 fusion.93
  28.7 1.3 compare_and_fusion.8
  30.0 0.6 gather_fusion
  30.7 0.7 compare_select_fusion.1
  31.6 1.9 %collective-permute-start.2 = (f32[5,1,1024]{2,1,0:T(1,128)S(1)}, f32[5,1,1024]{2,1,0:T(1,128)S(1)}, u32[]{:S(2)}, u32[]{:S(2)}) collective-permute-start(f32[5,1,1024]{2,1,0:T(1,128)S(1)} %slice.1233), channel_id=1, source_target_pairs={{0,1},{1,2},{2,3},{3,4},{4,5},{5,6},{6,7},{7,8},{8,9},{9,10},{10,1... | collective-permute-start | bytes 61448 | tf_op jit(solution)/shard_map/ppermute | solution.py:31
  33.6 2.4 %collective-permute-start.3 = (f32[5,1,1024]{2,1,0:T(1,128)S(1)}, f32[5,1,1024]{2,1,0:T(1,128)S(1)}, u32[]{:S(2)}, u32[]{:S(2)}) collective-permute-start(f32[5,1,1024]{2,1,0:T(1,128)S(1)} %copy.76), channel_id=1, source_target_pairs={{1,0},{2,1},{3,2},{4,3},{5,4},{6,5},{7,6},{8,7},{9,8},{10,9},{11,1... | collective-permute-start | bytes 61448 | tf_op jit(solution)/shard_map/ppermute | solution.py:32
  36.2 3.4 %collective-permute-done.3 = f32[5,1,1024]{2,1,0:T(1,128)S(1)} collective-permute-done((f32[5,1,1024]{2,1,0:T(1,128)S(1)}, f32[5,1,1024]{2,1,0:T(1,128)S(1)}, u32[]{:S(2)}, u32[]{:S(2)}) %collective-permute-start.3) | collective-permute-done | bytes 20512 | tf_op jit(solution)/shard_map/ppermute | solution.py:32
  40.0 1.9 %collective-permute-start.4 = (f32[1,1,1024]{2,1,0:T(1,128)S(1)}, f32[1,1,1024]{2,1,0:T(1,128)S(1)}, u32[]{:S(2)}, u32[]{:S(2)}) collective-permute-start(f32[1,1,1024]{2,1,0:T(1,128)S(1)} %get-tuple-element.288), channel_id=1, source_target_pairs={{0,1},{1,2},{2,3},{3,4},{4,5},{5,6},{6,7},{7,8},{8,9},{9,10},{10,1... | collective-permute-start | bytes 12296 | tf_op jit(solution)/shard_map/ppermute | solution.py:31
  42.0 2.4 %collective-permute-start.5 = (f32[1,1,1024]{2,1,0:T(1,128)S(1)}, f32[1,1,1024]{2,1,0:T(1,128)S(1)}, u32[]{:S(2)}, u32[]{:S(2)}) collective-permute-start(f32[1,1,1024]{2,1,0:T(1,128)S(1)} %get-tuple-element.289), channel_id=1, source_target_pairs={{1,0},{2,1},{3,2},{4,3},{5,4},{6,5},{7,6},{8,7},{9,8},{10,9},{11,1... | collective-permute-start | bytes 12296 | tf_op jit(solution)/shard_map/ppermute | solution.py:32
  44.4 0.7 fusion.94
  45.1 2.7 %collective-permute-done.5 = f32[1,1,1024]{2,1,0:T(1,128)S(1)} collective-permute-done((f32[1,1,1024]{2,1,0:T(1,128)S(1)}, f32[1,1,1024]{2,1,0:T(1,128)S(1)}, u32[]{:S(2)}, u32[]{:S(2)}) %collective-permute-start.5) | collective-permute-done | bytes 4128 | tf_op jit(solution)/shard_map/ppermute | solution.py:32
  48.2 1.9 %collective-permute-start.6 = (f32[1,1,1024]{2,1,0:T(1,128)S(1)}, f32[1,1,1024]{2,1,0:T(1,128)S(1)}, u32[]{:S(2)}, u32[]{:S(2)}) collective-permute-start(f32[1,1,1024]{2,1,0:T(1,128)S(1)} %get-tuple-element.286), channel_id=1, source_target_pairs={{0,1},{1,2},{2,3},{3,4},{4,5},{5,6},{6,7},{7,8},{8,9},{9,10},{10,1... | collective-permute-start | bytes 12296 | tf_op jit(solution)/shard_map/ppermute | solution.py:31
  50.1 2.4 %collective-permute-start.7 = (f32[1,1,1024]{2,1,0:T(1,128)S(1)}, f32[1,1,1024]{2,1,0:T(1,128)S(1)}, u32[]{:S(2)}, u32[]{:S(2)}) collective-permute-start(f32[1,1,1024]{2,1,0:T(1,128)S(1)} %get-tuple-element.287), channel_id=1, source_target_pairs={{1,0},{2,1},{3,2},{4,3},{5,4},{6,5},{7,6},{8,7},{9,8},{10,9},{11,1... | collective-permute-start | bytes 12296 | tf_op jit(solution)/shard_map/ppermute | solution.py:32
  52.5 3.4 %collective-permute-done.7 = f32[1,1,1024]{2,1,0:T(1,128)S(1)} collective-permute-done((f32[1,1,1024]{2,1,0:T(1,128)S(1)}, f32[1,1,1024]{2,1,0:T(1,128)S(1)}, u32[]{:S(2)}, u32[]{:S(2)}) %collective-permute-start.7) | collective-permute-done | bytes 4128 | tf_op jit(solution)/shard_map/ppermute | solution.py:32
  56.3 1.9 %collective-permute-start.8 = (f32[1,1,1024]{2,1,0:T(1,128)S(1)}, f32[1,1,1024]{2,1,0:T(1,128)S(1)}, u32[]{:S(2)}, u32[]{:S(2)}) collective-permute-start(f32[1,1,1024]{2,1,0:T(1,128)S(1)} %get-tuple-element.284), channel_id=1, source_target_pairs={{0,1},{1,2},{2,3},{3,4},{4,5},{5,6},{6,7},{7,8},{8,9},{9,10},{10,1... | collective-permute-start | bytes 12296 | tf_op jit(solution)/shard_map/ppermute | solution.py:31
  58.3 2.4 %collective-permute-start.9 = (f32[1,1,1024]{2,1,0:T(1,128)S(1)}, f32[1,1,1024]{2,1,0:T(1,128)S(1)}, u32[]{:S(2)}, u32[]{:S(2)}) collective-permute-start(f32[1,1,1024]{2,1,0:T(1,128)S(1)} %get-tuple-element.285), channel_id=1, source_target_pairs={{1,0},{2,1},{3,2},{4,3},{5,4},{6,5},{7,6},{8,7},{9,8},{10,9},{11,1... | collective-permute-start | bytes 12296 | tf_op jit(solution)/shard_map/ppermute | solution.py:32
  60.6 0.7 broadcast_compare_fusion
  61.3 2.8 %collective-permute-done.9 = f32[1,1,1024]{2,1,0:T(1,128)S(1)} collective-permute-done((f32[1,1,1024]{2,1,0:T(1,128)S(1)}, f32[1,1,1024]{2,1,0:T(1,128)S(1)}, u32[]{:S(2)}, u32[]{:S(2)}) %collective-permute-start.9) | collective-permute-done | bytes 4128 | tf_op jit(solution)/shard_map/ppermute | solution.py:32
  64.4 1.9 %collective-permute-start.10 = (f32[1,1,1024]{2,1,0:T(1,128)S(1)}, f32[1,1,1024]{2,1,0:T(1,128)S(1)}, u32[]{:S(2)}, u32[]{:S(2)}) collective-permute-start(f32[1,1,1024]{2,1,0:T(1,128)S(1)} %get-tuple-element.282), channel_id=1, source_target_pairs={{0,1},{1,2},{2,3},{3,4},{4,5},{5,6},{6,7},{7,8},{8,9},{9,10},{10,1... | collective-permute-start | bytes 12296 | tf_op jit(solution)/shard_map/ppermute | solution.py:31
  66.4 2.4 %collective-permute-start.11 = (f32[1,1,1024]{2,1,0:T(1,128)S(1)}, f32[1,1,1024]{2,1,0:T(1,128)S(1)}, u32[]{:S(2)}, u32[]{:S(2)}) collective-permute-start(f32[1,1,1024]{2,1,0:T(1,128)S(1)} %get-tuple-element.283), channel_id=1, source_target_pairs={{1,0},{2,1},{3,2},{4,3},{5,4},{6,5},{7,6},{8,7},{9,8},{10,9},{11,1... | collective-permute-start | bytes 12296 | tf_op jit(solution)/shard_map/ppermute | solution.py:32
  68.8 0.7 compare_and_fusion
  69.5 2.8 %collective-permute-done.11 = f32[1,1,1024]{2,1,0:T(1,128)S(1)} collective-permute-done((f32[1,1,1024]{2,1,0:T(1,128)S(1)}, f32[1,1,1024]{2,1,0:T(1,128)S(1)}, u32[]{:S(2)}, u32[]{:S(2)}) %collective-permute-start.11) | collective-permute-done | bytes 4128 | tf_op jit(solution)/shard_map/ppermute | solution.py:32
  72.6 1.9 %collective-permute-start.12 = (f32[1,1,1024]{2,1,0:T(1,128)S(1)}, f32[1,1,1024]{2,1,0:T(1,128)S(1)}, u32[]{:S(2)}, u32[]{:S(2)}) collective-permute-start(f32[1,1,1024]{2,1,0:T(1,128)S(1)} %get-tuple-element.280), channel_id=1, source_target_pairs={{0,1},{1,2},{2,3},{3,4},{4,5},{5,6},{6,7},{7,8},{8,9},{9,10},{10,1... | collective-permute-start | bytes 12296 | tf_op jit(solution)/shard_map/ppermute | solution.py:31
  74.5 2.4 %collective-permute-start.13 = (f32[1,1,1024]{2,1,0:T(1,128)S(1)}, f32[1,1,1024]{2,1,0:T(1,128)S(1)}, u32[]{:S(2)}, u32[]{:S(2)}) collective-permute-start(f32[1,1,1024]{2,1,0:T(1,128)S(1)} %get-tuple-element.281), channel_id=1, source_target_pairs={{1,0},{2,1},{3,2},{4,3},{5,4},{6,5},{7,6},{8,7},{9,8},{10,9},{11,1... | collective-permute-start | bytes 12296 | tf_op jit(solution)/shard_map/ppermute | solution.py:32
  76.9 0.7 compare_and_fusion.10
  78.2 2.1 %collective-permute-done.13 = f32[1,1,1024]{2,1,0:T(1,128)S(1)} collective-permute-done((f32[1,1,1024]{2,1,0:T(1,128)S(1)}, f32[1,1,1024]{2,1,0:T(1,128)S(1)}, u32[]{:S(2)}, u32[]{:S(2)}) %collective-permute-start.13) | collective-permute-done | bytes 4128 | tf_op jit(solution)/shard_map/ppermute | solution.py:32
  80.7 2.0 %collective-permute-start.14 = (f32[1,2,1024]{2,1,0:T(2,128)S(1)}, f32[1,2,1024]{2,1,0:T(2,128)S(1)}, u32[]{:S(2)}, u32[]{:S(2)}) collective-permute-start(f32[1,2,1024]{2,1,0:T(2,128)S(1)} %get-tuple-element.278), channel_id=1, source_target_pairs={{0,1},{1,2},{2,3},{3,4},{4,5},{5,6},{6,7},{7,8},{8,9},{9,10},{10,1... | collective-permute-start | bytes 24584 | tf_op jit(solution)/shard_map/ppermute | solution.py:21
  82.7 2.4 %collective-permute-start.15 = (f32[1,2,1024]{2,1,0:T(2,128)S(1)}, f32[1,2,1024]{2,1,0:T(2,128)S(1)}, u32[]{:S(2)}, u32[]{:S(2)}) collective-permute-start(f32[1,2,1024]{2,1,0:T(2,128)S(1)} %get-tuple-element.279), channel_id=1, source_target_pairs={{1,0},{2,1},{3,2},{4,3},{5,4},{6,5},{7,6},{8,7},{9,8},{10,9},{11,1... | collective-permute-start | bytes 24584 | tf_op jit(solution)/shard_map/ppermute | solution.py:21
  87.6 0.6 gather_fusion.1
  88.6 0.6 gather_fusion.5
  89.2 0.6 gather_fusion.4
  89.9 1.9 %collective-permute-start.17 = (f32[1,1,1024]{2,1,0:T(1,128)S(1)}, f32[1,1,1024]{2,1,0:T(1,128)S(1)}, u32[]{:S(2)}, u32[]{:S(2)}) collective-permute-start(f32[1,1,1024]{2,1,0:T(1,128)S(1)} %slice.1325), channel_id=1, source_target_pairs={{1,0},{2,1},{3,2},{4,3},{5,4},{6,5},{7,6},{8,7},{9,8},{10,9},{11,1... | collective-permute-start | bytes 12296 | tf_op jit(solution)/shard_map/ppermute | solution.py:21
  91.8 4.5 %collective-permute-start.16 = (f32[1,1,1024]{2,1,0:T(1,128)S(1)}, f32[1,1,1024]{2,1,0:T(1,128)S(1)}, u32[]{:S(2)}, u32[]{:S(2)}) collective-permute-start(f32[1,1,1024]{2,1,0:T(1,128)S(1)} %dynamic-slice_bitcast_fusion), channel_id=1, source_target_pairs={{0,1},{1,2},{2,3},{3,4},{4,5},{5,6},{6,7},{7,8},{8,9},{9,10},{10,1... | collective-permute-start | bytes 12296 | tf_op jit(solution)/shard_map/ppermute | solution.py:21
  99.1 1.3 scatter.24
  100.4 6.7 %scatter.25 = f32[24,22,1024]{2,1,0:T(8,128)S(1)} dynamic-update-slice(f32[24,22,1024]{2,1,0:T(8,128)S(1)} %scatter.24, f32[24,16,1024]{2,1,0:T(8,128)} %copy-done, s32[]{:T(128)} %constant.341.clone.1, s32[]{:T(128)} %constant.339.clone.1, s32[]{:T(128)} %constant.341.clone.1) | dynamic-update-slice | bytes 3145732 | tf_op jit(solution)/shard_map/scatter | solution.py:140
  107.1 1.4 %dynamic_update_slice.10 = f32[24,22,1024]{2,1,0:T(8,128)S(1)} dynamic-update-slice(f32[24,22,1024]{2,1,0:T(8,128)S(1)} %scatter.25, f32[24,3,1024]{2,1,0:T(4,128)S(1)} %collective-permute-done.19, s32[]{:T(128)} %constant.341.clone.1, s32[]{:T(128)S(6)} %select_n.214, s32[]{:T(128)} %constant.341.clone.1) | dynamic-update-slice | bytes 589828 | tf_op jit(solution)/shard_map/dynamic_update_slice | solution.py:141
  108.5 0.8 slice_bitcast_fusion.21
  109.8 0.9 multiply_subtract_fusion.2
  111.2 0.6 slice.1362
  111.9 0.8 fusion.130
  112.7 0.9 fusion.128
  113.6 3.7 %collective-permute-start.20 = (f32[3,2,1024]{2,1,0:T(2,128)S(1)}, f32[3,2,1024]{2,1,0:T(2,128)S(1)}, u32[]{:S(2)}, u32[]{:S(2)}) collective-permute-start(f32[3,2,1024]{2,1,0:T(2,128)S(1)} %constant_dynamic-slice_fusion), channel_id=1, source_target_pairs={{0,1},{1,2},{2,3},{3,4},{4,5},{5,6},{6,7},{7,8},{8,9},{9,10},{10,1... | collective-permute-start | bytes 73736 | tf_op jit(solution)/shard_map/ppermute | solution.py:21
  117.3 2.1 %collective-permute-start.21 = (f32[3,2,1024]{2,1,0:T(2,128)}, f32[3,2,1024]{2,1,0:T(2,128)}, u32[]{:S(2)}, u32[]{:S(2)}) collective-permute-start(f32[3,2,1024]{2,1,0:T(2,128)} %slice.1362), channel_id=1, source_target_pairs={{1,0},{2,1},{3,2},{4,3},{5,4},{6,5},{7,6},{8,7},{9,8},{10,9},{11,1... | collective-permute-start | bytes 73736 | tf_op jit(solution)/shard_map/ppermute | solution.py:21
  119.4 0.9 fusion.129
  120.4 0.6 scatter.29
  121.0 2.7 %collective-permute-done.21 = f32[3,2,1024]{2,1,0:T(2,128)} collective-permute-done((f32[3,2,1024]{2,1,0:T(2,128)}, f32[3,2,1024]{2,1,0:T(2,128)}, u32[]{:S(2)}, u32[]{:S(2)}) %collective-permute-start.21) | collective-permute-done | bytes 24608 | tf_op jit(solution)/shard_map/ppermute | solution.py:21
  123.7 1.0 dynamic_update_slice.11
  124.7 1.8 %fusion.3 = f32[3,22,1024]{2,1,0:T(8,128)S(1)} fusion(f32[1,22,1024]{2,1,0:T(8,128)} %get-tuple-element.189, f32[1,22,1024]{2,1,0:T(8,128)} %get-tuple-element.184, f32[1,22,1024]{2,1,0:T(8,128)} %get-tuple-element.186, f32[3,22,1023]{2,1,0:T(8,128)} %get-tuple-element.257, f32[3,22,1023]{2,1,0:T(8,128)S(1)} %get-tuple-element.256, ...), kind=kLoop, calls=%fused_computation.35 | loop fusion | flops 1148928 | bytes 3021830 | tf_op jit(solution)/shard_map/sub | solution.py:257
  133.3 0.8 fusion.18
  (198 shorter events, 13.7 us)
Async XLA Ops:
  0.0 8.6 %copy-start.11 = (f32[3,16,1024]{2,1,0:T(8,128)S(1)}, f32[3,16,1024]{2,1,0:T(8,128)}, u32[]{:S(2)}) copy-start(f32[3,16,1024]{2,1,0:T(8,128)} %param.30) | copy-start | bytes 589828
  0.0 8.9 %copy-start.13 = (f32[3,16,1024]{2,1,0:T(8,128)S(1)}, f32[3,16,1024]{2,1,0:T(8,128)}, u32[]{:S(2)}) copy-start(f32[3,16,1024]{2,1,0:T(8,128)} %param.27) | copy-start | bytes 589828
  0.0 9.0 %copy-start.1 = (f32[2,16,1024]{2,1,0:T(8,128)S(1)}, f32[2,16,1024]{2,1,0:T(8,128)}, u32[]{:S(2)}) copy-start(f32[2,16,1024]{2,1,0:T(8,128)} %param.31) | copy-start | bytes 393220
  9.0 21.6 %copy-start = (f32[24,16,1024]{2,1,0:T(8,128)}, f32[24,16,1024]{2,1,0:T(8,128)S(1)}, u32[]{:S(2)}) copy-start(f32[24,16,1024]{2,1,0:T(8,128)S(1)} %get-tuple-element.129) | copy-start | bytes 4718596
  10.2 21.3 %collective-permute-start.1 = (f32[6,2,1024]{2,1,0:T(2,128)S(1)}, f32[6,2,1024]{2,1,0:T(2,128)S(1)}, u32[]{:S(2)}, u32[]{:S(2)}) collective-permute-start(f32[6,2,1024]{2,1,0:T(2,128)S(1)} %bitcast_select_fusion), channel_id=1, source_target_pairs={{1,0},{2,1},{3,2},{4,3},{5,4},{6,5},{7,6},{8,7},{9,8},{10,9},{11,1... | collective-permute-start | bytes 147464 | tf_op jit(solution)/shard_map/ppermute | solution.py:21
  14.8 16.6 %collective-permute-start = (f32[6,2,1024]{2,1,0:T(2,128)S(1)}, f32[6,2,1024]{2,1,0:T(2,128)S(1)}, u32[]{:S(2)}, u32[]{:S(2)}) collective-permute-start(f32[6,2,1024]{2,1,0:T(2,128)S(1)} %bitcast_select_fusion.1), channel_id=1, source_target_pairs={{0,1},{1,2},{2,3},{3,4},{4,5},{5,6},{6,7},{7,8},{8,9},{9,10},{10,1... | collective-permute-start | bytes 147464 | tf_op jit(solution)/shard_map/ppermute | solution.py:21
  20.9 86.2 %collective-permute-start.19 = (f32[24,3,1024]{2,1,0:T(4,128)S(1)}, f32[24,3,1024]{2,1,0:T(4,128)S(1)}, u32[]{:S(2)}, u32[]{:S(2)}) collective-permute-start(f32[24,3,1024]{2,1,0:T(4,128)S(1)} %get-tuple-element.192), channel_id=1, source_target_pairs={{1,0},{2,1},{3,2},{4,3},{5,4},{6,5},{7,6},{8,7},{9,8},{10,9},{11,1... | collective-permute-start | bytes 884744 | tf_op jit(solution)/shard_map/ppermute | solution.py:21
  22.8 76.2 %collective-permute-start.18 = (f32[24,3,1024]{2,1,0:T(4,128)}, f32[24,3,1024]{2,1,0:T(4,128)}, u32[]{:S(2)}, u32[]{:S(2)}) collective-permute-start(f32[24,3,1024]{2,1,0:T(4,128)} %get-tuple-element.193), channel_id=1, source_target_pairs={{0,1},{1,2},{2,3},{3,4},{4,5},{5,6},{6,7},{7,8},{8,9},{9,10},{10,1... | collective-permute-start | bytes 884744 | tf_op jit(solution)/shard_map/ppermute | solution.py:21
  31.6 4.6 %collective-permute-start.2 = (f32[5,1,1024]{2,1,0:T(1,128)S(1)}, f32[5,1,1024]{2,1,0:T(1,128)S(1)}, u32[]{:S(2)}, u32[]{:S(2)}) collective-permute-start(f32[5,1,1024]{2,1,0:T(1,128)S(1)} %slice.1233), channel_id=1, source_target_pairs={{0,1},{1,2},{2,3},{3,4},{4,5},{5,6},{6,7},{7,8},{8,9},{9,10},{10,1... | collective-permute-start | bytes 61448 | tf_op jit(solution)/shard_map/ppermute | solution.py:31
  33.6 6.0 %collective-permute-start.3 = (f32[5,1,1024]{2,1,0:T(1,128)S(1)}, f32[5,1,1024]{2,1,0:T(1,128)S(1)}, u32[]{:S(2)}, u32[]{:S(2)}) collective-permute-start(f32[5,1,1024]{2,1,0:T(1,128)S(1)} %copy.76), channel_id=1, source_target_pairs={{1,0},{2,1},{3,2},{4,3},{5,4},{6,5},{7,6},{8,7},{9,8},{10,9},{11,1... | collective-permute-start | bytes 61448 | tf_op jit(solution)/shard_map/ppermute | solution.py:32
  40.0 5.0 %collective-permute-start.4 = (f32[1,1,1024]{2,1,0:T(1,128)S(1)}, f32[1,1,1024]{2,1,0:T(1,128)S(1)}, u32[]{:S(2)}, u32[]{:S(2)}) collective-permute-start(f32[1,1,1024]{2,1,0:T(1,128)S(1)} %get-tuple-element.288), channel_id=1, source_target_pairs={{0,1},{1,2},{2,3},{3,4},{4,5},{5,6},{6,7},{7,8},{8,9},{9,10},{10,1... | collective-permute-start | bytes 12296 | tf_op jit(solution)/shard_map/ppermute | solution.py:31
  42.0 5.8 %collective-permute-start.5 = (f32[1,1,1024]{2,1,0:T(1,128)S(1)}, f32[1,1,1024]{2,1,0:T(1,128)S(1)}, u32[]{:S(2)}, u32[]{:S(2)}) collective-permute-start(f32[1,1,1024]{2,1,0:T(1,128)S(1)} %get-tuple-element.289), channel_id=1, source_target_pairs={{1,0},{2,1},{3,2},{4,3},{5,4},{6,5},{7,6},{8,7},{9,8},{10,9},{11,1... | collective-permute-start | bytes 12296 | tf_op jit(solution)/shard_map/ppermute | solution.py:32
  48.2 4.4 %collective-permute-start.6 = (f32[1,1,1024]{2,1,0:T(1,128)S(1)}, f32[1,1,1024]{2,1,0:T(1,128)S(1)}, u32[]{:S(2)}, u32[]{:S(2)}) collective-permute-start(f32[1,1,1024]{2,1,0:T(1,128)S(1)} %get-tuple-element.286), channel_id=1, source_target_pairs={{0,1},{1,2},{2,3},{3,4},{4,5},{5,6},{6,7},{7,8},{8,9},{9,10},{10,1... | collective-permute-start | bytes 12296 | tf_op jit(solution)/shard_map/ppermute | solution.py:31
  50.1 5.8 %collective-permute-start.7 = (f32[1,1,1024]{2,1,0:T(1,128)S(1)}, f32[1,1,1024]{2,1,0:T(1,128)S(1)}, u32[]{:S(2)}, u32[]{:S(2)}) collective-permute-start(f32[1,1,1024]{2,1,0:T(1,128)S(1)} %get-tuple-element.287), channel_id=1, source_target_pairs={{1,0},{2,1},{3,2},{4,3},{5,4},{6,5},{7,6},{8,7},{9,8},{10,9},{11,1... | collective-permute-start | bytes 12296 | tf_op jit(solution)/shard_map/ppermute | solution.py:32
  56.3 5.0 %collective-permute-start.8 = (f32[1,1,1024]{2,1,0:T(1,128)S(1)}, f32[1,1,1024]{2,1,0:T(1,128)S(1)}, u32[]{:S(2)}, u32[]{:S(2)}) collective-permute-start(f32[1,1,1024]{2,1,0:T(1,128)S(1)} %get-tuple-element.284), channel_id=1, source_target_pairs={{0,1},{1,2},{2,3},{3,4},{4,5},{5,6},{6,7},{7,8},{8,9},{9,10},{10,1... | collective-permute-start | bytes 12296 | tf_op jit(solution)/shard_map/ppermute | solution.py:31
  58.3 5.8 %collective-permute-start.9 = (f32[1,1,1024]{2,1,0:T(1,128)S(1)}, f32[1,1,1024]{2,1,0:T(1,128)S(1)}, u32[]{:S(2)}, u32[]{:S(2)}) collective-permute-start(f32[1,1,1024]{2,1,0:T(1,128)S(1)} %get-tuple-element.285), channel_id=1, source_target_pairs={{1,0},{2,1},{3,2},{4,3},{5,4},{6,5},{7,6},{8,7},{9,8},{10,9},{11,1... | collective-permute-start | bytes 12296 | tf_op jit(solution)/shard_map/ppermute | solution.py:32
  64.4 5.0 %collective-permute-start.10 = (f32[1,1,1024]{2,1,0:T(1,128)S(1)}, f32[1,1,1024]{2,1,0:T(1,128)S(1)}, u32[]{:S(2)}, u32[]{:S(2)}) collective-permute-start(f32[1,1,1024]{2,1,0:T(1,128)S(1)} %get-tuple-element.282), channel_id=1, source_target_pairs={{0,1},{1,2},{2,3},{3,4},{4,5},{5,6},{6,7},{7,8},{8,9},{9,10},{10,1... | collective-permute-start | bytes 12296 | tf_op jit(solution)/shard_map/ppermute | solution.py:31
  66.4 5.8 %collective-permute-start.11 = (f32[1,1,1024]{2,1,0:T(1,128)S(1)}, f32[1,1,1024]{2,1,0:T(1,128)S(1)}, u32[]{:S(2)}, u32[]{:S(2)}) collective-permute-start(f32[1,1,1024]{2,1,0:T(1,128)S(1)} %get-tuple-element.283), channel_id=1, source_target_pairs={{1,0},{2,1},{3,2},{4,3},{5,4},{6,5},{7,6},{8,7},{9,8},{10,9},{11,1... | collective-permute-start | bytes 12296 | tf_op jit(solution)/shard_map/ppermute | solution.py:32
  72.6 5.7 %collective-permute-start.12 = (f32[1,1,1024]{2,1,0:T(1,128)S(1)}, f32[1,1,1024]{2,1,0:T(1,128)S(1)}, u32[]{:S(2)}, u32[]{:S(2)}) collective-permute-start(f32[1,1,1024]{2,1,0:T(1,128)S(1)} %get-tuple-element.280), channel_id=1, source_target_pairs={{0,1},{1,2},{2,3},{3,4},{4,5},{5,6},{6,7},{7,8},{8,9},{9,10},{10,1... | collective-permute-start | bytes 12296 | tf_op jit(solution)/shard_map/ppermute | solution.py:31
  74.5 5.8 %collective-permute-start.13 = (f32[1,1,1024]{2,1,0:T(1,128)S(1)}, f32[1,1,1024]{2,1,0:T(1,128)S(1)}, u32[]{:S(2)}, u32[]{:S(2)}) collective-permute-start(f32[1,1,1024]{2,1,0:T(1,128)S(1)} %get-tuple-element.281), channel_id=1, source_target_pairs={{1,0},{2,1},{3,2},{4,3},{5,4},{6,5},{7,6},{8,7},{9,8},{10,9},{11,1... | collective-permute-start | bytes 12296 | tf_op jit(solution)/shard_map/ppermute | solution.py:32
  80.7 8.4 %collective-permute-start.14 = (f32[1,2,1024]{2,1,0:T(2,128)S(1)}, f32[1,2,1024]{2,1,0:T(2,128)S(1)}, u32[]{:S(2)}, u32[]{:S(2)}) collective-permute-start(f32[1,2,1024]{2,1,0:T(2,128)S(1)} %get-tuple-element.278), channel_id=1, source_target_pairs={{0,1},{1,2},{2,3},{3,4},{4,5},{5,6},{6,7},{7,8},{8,9},{9,10},{10,1... | collective-permute-start | bytes 24584 | tf_op jit(solution)/shard_map/ppermute | solution.py:21
  82.7 5.9 %collective-permute-start.15 = (f32[1,2,1024]{2,1,0:T(2,128)S(1)}, f32[1,2,1024]{2,1,0:T(2,128)S(1)}, u32[]{:S(2)}, u32[]{:S(2)}) collective-permute-start(f32[1,2,1024]{2,1,0:T(2,128)S(1)} %get-tuple-element.279), channel_id=1, source_target_pairs={{1,0},{2,1},{3,2},{4,3},{5,4},{6,5},{7,6},{8,7},{9,8},{10,9},{11,1... | collective-permute-start | bytes 24584 | tf_op jit(solution)/shard_map/ppermute | solution.py:21
  89.9 9.1 %collective-permute-start.17 = (f32[1,1,1024]{2,1,0:T(1,128)S(1)}, f32[1,1,1024]{2,1,0:T(1,128)S(1)}, u32[]{:S(2)}, u32[]{:S(2)}) collective-permute-start(f32[1,1,1024]{2,1,0:T(1,128)S(1)} %slice.1325), channel_id=1, source_target_pairs={{1,0},{2,1},{3,2},{4,3},{5,4},{6,5},{7,6},{8,7},{9,8},{10,9},{11,1... | collective-permute-start | bytes 12296 | tf_op jit(solution)/shard_map/ppermute | solution.py:21
  91.8 6.6 %collective-permute-start.16 = (f32[1,1,1024]{2,1,0:T(1,128)S(1)}, f32[1,1,1024]{2,1,0:T(1,128)S(1)}, u32[]{:S(2)}, u32[]{:S(2)}) collective-permute-start(f32[1,1,1024]{2,1,0:T(1,128)S(1)} %dynamic-slice_bitcast_fusion), channel_id=1, source_target_pairs={{0,1},{1,2},{2,3},{3,4},{4,5},{5,6},{6,7},{7,8},{8,9},{9,10},{10,1... | collective-permute-start | bytes 12296 | tf_op jit(solution)/shard_map/ppermute | solution.py:21
  99.0 10.2 %copy-start.9 = (f32[1,22,1024]{2,1,0:T(8,128)}, f32[1,22,1024]{2,1,0:T(8,128)S(1)}, u32[]{:S(2)}) copy-start(f32[1,22,1024]{2,1,0:T(8,128)S(1)} %dynamic_update_slice.9) | copy-start | bytes 270340
  109.3 2.5 %copy-start.2 = (f32[1,22,1024]{2,1,0:T(8,128)}, f32[1,22,1024]{2,1,0:T(8,128)S(1)}, u32[]{:S(2)}) copy-start(f32[1,22,1024]{2,1,0:T(8,128)S(1)} %get-tuple-element.185) | copy-start | bytes 270340
  109.3 2.5 %copy-start.3 = (f32[1,22,1024]{2,1,0:T(8,128)}, f32[1,22,1024]{2,1,0:T(8,128)S(1)}, u32[]{:S(2)}) copy-start(f32[1,22,1024]{2,1,0:T(8,128)S(1)} %get-tuple-element.187) | copy-start | bytes 270340
  109.3 2.5 %copy-start.4 = (f32[1,22,1024]{2,1,0:T(8,128)}, f32[1,22,1024]{2,1,0:T(8,128)S(1)}, u32[]{:S(2)}) copy-start(f32[1,22,1024]{2,1,0:T(8,128)S(1)} %get-tuple-element.188) | copy-start | bytes 270340
  113.6 6.8 %collective-permute-start.20 = (f32[3,2,1024]{2,1,0:T(2,128)S(1)}, f32[3,2,1024]{2,1,0:T(2,128)S(1)}, u32[]{:S(2)}, u32[]{:S(2)}) collective-permute-start(f32[3,2,1024]{2,1,0:T(2,128)S(1)} %constant_dynamic-slice_fusion), channel_id=1, source_target_pairs={{0,1},{1,2},{2,3},{3,4},{4,5},{5,6},{6,7},{7,8},{8,9},{9,10},{10,1... | collective-permute-start | bytes 73736 | tf_op jit(solution)/shard_map/ppermute | solution.py:21
  117.3 6.4 %collective-permute-start.21 = (f32[3,2,1024]{2,1,0:T(2,128)}, f32[3,2,1024]{2,1,0:T(2,128)}, u32[]{:S(2)}, u32[]{:S(2)}) collective-permute-start(f32[3,2,1024]{2,1,0:T(2,128)} %slice.1362), channel_id=1, source_target_pairs={{1,0},{2,1},{3,2},{4,3},{5,4},{6,5},{7,6},{8,7},{9,8},{10,9},{11,1... | collective-permute-start | bytes 73736 | tf_op jit(solution)/shard_map/ppermute | solution.py:21
  121.0 5.6 %copy-start.5 = (f32[22,1024]{1,0:T(8,128)S(1)}, f32[22,1024]{1,0:T(8,128)}, u32[]{:S(2)}) copy-start(f32[22,1024]{1,0:T(8,128)} %get-tuple-element.124) | copy-start | bytes 270340
  121.0 5.6 %copy-start.6 = (f32[22,1024]{1,0:T(8,128)S(1)}, f32[22,1024]{1,0:T(8,128)}, u32[]{:S(2)}) copy-start(f32[22,1024]{1,0:T(8,128)} %get-tuple-element.125) | copy-start | bytes 270340
  124.7 1.9 %copy-start.7 = (f32[22,1024]{1,0:T(8,128)S(1)}, f32[22,1024]{1,0:T(8,128)}, u32[]{:S(2)}) copy-start(f32[22,1024]{1,0:T(8,128)} %get-tuple-element.126) | copy-start | bytes 270340
  124.7 1.9 %copy-start.8 = (f32[22,1024]{1,0:T(8,128)S(1)}, f32[22,1024]{1,0:T(8,128)}, u32[]{:S(2)}) copy-start(f32[22,1024]{1,0:T(8,128)} %get-tuple-element.127) | copy-start | bytes 270340
  124.7 1.9 %copy-start.12 = (f32[22,1024]{1,0:T(8,128)S(1)}, f32[22,1024]{1,0:T(8,128)}, u32[]{:S(2)}) copy-start(f32[22,1024]{1,0:T(8,128)} %get-tuple-element.123) | copy-start | bytes 270340
  132.4 0.9 copy-start.10
where the time goes:
time: 135 us; the launch traced here: 134 us
  starting transfers between devices  55.5 us (41%)
  other arithmetic  30.1 us (22%)
  local copies, waits for them, and re-layouts  20.5 us (15%)
  waiting for transfers between devices  20.3 us (15%)
  between operations  7.7 us (6%)
    ppermute x10, starting transfers between devices, from_behind(): return lax.ppermute(block, axis, route)  29.5 us
    ppermute x6, waiting for transfers between devices, with_halo(): after = lax.ppermute(first, axis, down)  17.2 us
    ppermute x6, starting transfers between devices, with_halo(): after = lax.ppermute(first, axis, down)  14.3 us
    ppermute x6, starting transfers between devices, with_halo(): before = lax.ppermute(last, axis, up)  11.6 us
    scatter x3, local copies, waits for them, and re-layouts, ragged_halo(): extended = extended.at[:, 3:3 + values.shape[1]].set(values)  7.67 us
    slice x24, other arithmetic, lane_next(): values[..., stride:]  4.3 us
    and x3, other arithmetic, gather_planes(): picked = jnp.take(packed, jnp.clip(local_ids, 0, CAP - 1), axis=1)  3.87 us
    sub x6, other arithmetic, on_device(): target - fine_apply(local, sub_accum, sub_mobility, sub_plane, sub_row, s...  3.78 us
  transfers between devices with their start and end apart: 22, of which 8 were waited for; matrix products, arithmetic and copies ran while one was open for 18% of the time, Pallas kernels for 0%

commit v1 on v0

v1 whole, which is shorter than its diff:
```python
import functools

import jax
import jax.numpy as jnp
from jax import lax
from jax.experimental import pallas as pl
from jax.experimental.pallas import tpu as pltpu
from jax.sharding import PartitionSpec as P

CX = 8
NZ = 32
CHEB = 6
SWEEPS = 6
CAP = 16
CHEB_LOW = 0.1
CHEB_HIGH = 2.0

LEAD = 7
OWN = LEAD + CAP
PW = 30
FW = 18
SW = 16
HALO = 11


def y_next(x, lane):
    r = pltpu.roll(x, 96, x.ndim - 1)
    return jnp.where(lane < 96, r, pltpu.roll(r, 7, x.ndim - 2))


def y_prev(x, lane):
    r = pltpu.roll(x, 32, x.ndim - 1)
    return jnp.where(lane >= 32, r, pltpu.roll(r, 1, x.ndim - 2))


def z_next(x):
    return pltpu.roll(x, 127, x.ndim - 1)


def z_prev(x):
    return pltpu.roll(x, 1, x.ndim - 1)


def kernel(
    n,
    counts,
    resid,
    accum,
    mobility,
    trans,
    decouple,
    out,
    own,
    pown,
    below1,
    above1,
    below2,
    above2,
    fup,
    fbelow,
    fabove,
    pw,
    coef,
    direction,
    remain,
    total,
    fine,
    blocks,
    carried,
    target,
    result,
    send_sem,
    recv_sem,
):
    me = lax.axis_index("gx")
    grid = CX * n
    barrier = pltpu.get_barrier_semaphore()
    here = {}
    for step in (-2, -1, 1, 2):
        here[step] = (me + step >= 0) & (me + step < n)

        @pl.when(here[step])
        def _():
            pl.semaphore_signal(
                barrier, inc=1, device_id={"gx": me + step}, device_id_type=pl.DeviceIdType.MESH
            )

    start = jnp.int32(0)
    for part in range(n):
        start = start + jnp.where(part < me, counts[part], 0)
    count = counts[me]
    end = start + count
    base = CX * me
    drift = jnp.clip(start - base, -2, 2)
    drift_end = jnp.clip(end - base - CX, -2, 2)

    shape = (1, 8, 128)
    lane = lax.broadcasted_iota(jnp.int32, shape, 2)
    row = lax.broadcasted_iota(jnp.int32, shape, 1)
    keep_row = jnp.where((row < 7) | (lane < 96), 1.0, 0.0)
    keep_lane = jnp.where(lane % NZ < NZ - 1, 1.0, 0.0)

    def planes(first, length):
        return first + lax.broadcasted_iota(jnp.int32, (length, 8, 128), 0)

    blank = jnp.zeros((LEAD, 8, 128), jnp.float32)
    order = [(mobility, i) for i in range(9)] + [(accum, i) for i in range(9)]
    order += [(resid, i) for i in range(3)] + [(trans, i) for i in range(3)]
    order += [(decouple, i) for i in range(2)]
    spans = [(mobility, 0, 9), (accum, 9, 9), (resid, 18, 3), (trans, 21, 3), (decouple, 24, 2)]
    for ref, first, length in spans:

        def place(i, _, ref=ref, first=first):
            own[first + i, :LEAD] = blank
            own[first + i, LEAD:] = ref[i].reshape(CAP, 8, 128)
            return 0

        lax.fori_loop(0, length, place, 0)

    at = 5 - drift
    spot = planes(base - 2, 12)
    mine = (spot >= start) & (spot < end)

    def field(i):
        return own[i, pl.ds(at, 12)]

    one, two = field(24), field(25)
    pown[0] = jnp.where(mine, field(18) + one * field(19) + two * field(20), 0.0)
    pown[1] = jnp.where(mine, field(0) + one * field(3) + two * field(6), 0.0)
    pown[2] = jnp.where(mine, field(9) + one * field(12) + two * field(15), 0.0)
    pown[3] = jnp.where(mine & (spot < grid - 1), field(21), 0.0)
    pown[4] = jnp.where(mine, field(22) * keep_row, 0.0)
    pown[5] = jnp.where(mine, field(23) * keep_lane, 0.0)

    for i in range(21):
        fup[i] = own[i, pl.ds(LEAD + jnp.clip(count, 4, 12) - 3, 3)]

    for step, ref in ((-1, below1), (1, above1), (-2, below2), (2, above2)):

        @pl.when(jnp.logical_not(here[step]))
        def _():
            ref[...] = jnp.zeros_like(ref)

    known = jnp.int32(0)
    for step in here:
        known = known + here[step].astype(jnp.int32)
    pl.semaphore_wait(barrier, known)

    def send(src, dst, step, slot):
        return pltpu.make_async_remote_copy(
            src_ref=src,
            dst_ref=dst,
            send_sem=send_sem.at[slot],
            recv_sem=recv_sem.at[slot],
            device_id={"gx": me + step},
            device_id_type=pl.DeviceIdType.MESH,
        )

    copies = [
        (1, send(pown, below1, 1, 0)),
        (-1, send(pown, above1, -1, 1)),
        (2, send(pown.at[:, 7:12], below2, 2, 2)),
        (-2, send(pown.at[:, 0:5], above2, -2, 3)),
        (1, send(fup, fbelow.at[:, 4:7], 1, 4)),
        (-1, send(own.at[0:21, LEAD : LEAD + 3], fabove.at[:, 4:7], -1, 5)),
    ]
    for step, copy in copies:

        @pl.when(here[step])
        def _():
            copy.start()

    for step, copy in copies[:4]:

        @pl.when(here[-step])
        def _():
            copy.wait_recv()

    for i in range(6):
        pw[i, 0:1] = below2[i, 0:1]
        pw[i, 1:5] = below2[i, 1:5] + below1[i, 0:4]
        pw[i, 5:9] = below1[i, 4:8]
        pw[i, 9:13] = below1[i, 8:12] + pown[i, 0:4]
        pw[i, 13:17] = pown[i, 4:8]
        pw[i, 17:21] = pown[i, 8:12] + above1[i, 0:4]
        pw[i, 21:25] = above1[i, 4:8]
        pw[i, 25:29] = above1[i, 8:12] + above2[i, 0:4]
        pw[i, 29:30] = above2[i, 4:5]
    zero = jnp.zeros((1, 8, 128), jnp.float32)
    for i in range(2):
        direction[i, 0:1] = zero
        direction[i, PW - 1 : PW] = zero

    middle = 0.5 * (CHEB_HIGH + CHEB_LOW)
    radius = 0.5 * (CHEB_HIGH - CHEB_LOW)
    aspect = middle / radius
    PC = 4

    def prepare(j, _):
        k = 1 + j * PC
        lam = pw[1, pl.ds(k, PC)]
        lam_up = pw[1, pl.ds(k + 1, PC)]
        lam_down = pw[1, pl.ds(k - 1, PC)]
        tx_down = pw[3, pl.ds(k - 1, PC)]
        cx = pw[3, pl.ds(k, PC)] * (lam + lam_up) * 0.5
        cx_down = tx_down * (lam_down + lam) * 0.5
        cy = pw[4, pl.ds(k, PC)] * (lam + y_next(lam, lane)) * 0.5
        cz = pw[5, pl.ds(k, PC)] * (lam + z_next(lam)) * 0.5
        cy_down = y_prev(cy, lane)
        cz_down = z_prev(cz)
        pivot = pw[2, pl.ds(k, PC)] + cx + cx_down + cy + cy_down + cz + cz_down
        where = planes(base - 11 + k, PC)
        inverse = 1.0 / jnp.where((where >= 0) & (where < grid), pivot, 1.0)
        for i, value in enumerate((cx, cx_down, cy, cy_down, cz, cz_down)):
            coef[i, pl.ds(k, PC)] = value * inverse
        scaled = pw[0, pl.ds(k, PC)] * inverse
        remain[pl.ds(k, PC)] = scaled
        first = scaled / middle
        direction[0, pl.ds(k, PC)] = first
        total[pl.ds(k, PC)] = first
        return 0

    lax.fori_loop(0, (PW - 2) // PC, prepare, 0)

    factor = 1.0 / aspect
    for iteration in range(CHEB - 1):
        now, later = iteration % 2, (iteration + 1) % 2
        factor_next = 1.0 / (2.0 * aspect - factor)

        def advance(j, _, now=now, later=later, factor=factor, factor_next=factor_next):
            k = 1 + j * PC
            d = direction[now, pl.ds(k, PC)]
            across = coef[0, pl.ds(k, PC)] * direction[now, pl.ds(k + 1, PC)]
            across = across + coef[1, pl.ds(k, PC)] * direction[now, pl.ds(k - 1, PC)]
            across = across + coef[2, pl.ds(k, PC)] * y_next(d, lane)
            across = across + coef[3, pl.ds(k, PC)] * y_prev(d, lane)
            across = across + coef[4, pl.ds(k, PC)] * z_next(d)
            across = across + coef[5, pl.ds(k, PC)] * z_prev(d)
            e = remain[pl.ds(k, PC)] - d + across
            remain[pl.ds(k, PC)] = e
            d = (factor_next * factor) * d + (2.0 * factor_next / radius) * e
            direction[later, pl.ds(k, PC)] = d
            total[pl.ds(k, PC)] = total[pl.ds(k, PC)] + d
            return 0

        lax.fori_loop(0, (PW - 2) // PC, advance, 0)
        factor = factor_next

    for step, copy in copies[4:]:

        @pl.when(here[-step])
        def _():
            copy.wait_recv()

    at_own = 2 - drift
    at_below = 2 - drift
    at_above = 2 - drift_end
    spot_low = planes(base - 5, 7)
    spot_mid = planes(base + 2, 4)
    spot_high = planes(base + 6, 7)

    def owned(spot):
        return (spot >= start) & (spot < end)

    low_mine, mid_mine, high_mine = owned(spot_low), owned(spot_mid), owned(spot_high)
    low_near = (spot_low >= start - 3) & (spot_low < start) & (spot_low >= 0)
    high_near = (spot_high >= end) & (spot_high < end + 3) & (spot_high < grid)

    def assemble(i, _):
        low = jnp.where(low_near, fbelow[i, pl.ds(at_below, 7)], 0.0)
        high = jnp.where(high_near, fabove[i, pl.ds(at_above, 7)], 0.0)
        fine[i, 0:7] = jnp.where(low_mine, own[i, pl.ds(at_own, 7)], low)
        fine[i, 7:11] = jnp.where(mid_mine, own[i, pl.ds(at_own + 7, 4)], 0.0)
        fine[i, 11:18] = jnp.where(high_mine, own[i, pl.ds(at_own + 11, 7)], high)
        return 0

    lax.fori_loop(0, 21, assemble, 0)

    for i in range(3):
        for slot in range(2):
            carried[slot, i, 0:1] = zero
            carried[slot, i, FW - 1 : FW] = zero
        carried[1, i] = fine[3 * i] * total[6 : 6 + FW]

    def across_of(slot, k, size):
        tx = pw[3, pl.ds(k + 6, size)]
        tx_down = pw[3, pl.ds(k + 5, size)]
        ty = pw[4, pl.ds(k + 6, size)]
        tz = pw[5, pl.ds(k + 6, size)]
        ty_down = y_prev(ty, lane)
        tz_down = z_prev(tz)
        sums = []
        for i in range(3):
            u = carried[slot, i, pl.ds(k, size)]
            value = tx * carried[slot, i, pl.ds(k + 1, size)]
            value = value + tx_down * carried[slot, i, pl.ds(k - 1, size)]
            value = value + ty * y_next(u, lane) + ty_down * y_prev(u, lane)
            value = value + tz * z_next(u) + tz_down * z_prev(u)
            sums.append(value)
        return sums, tx + tx_down + ty + ty_down + tz + tz_down

    def times(first, k, size, vector):
        return [
            blocks[first + 3 * i, pl.ds(k, size)] * vector[0]
            + blocks[first + 3 * i + 1, pl.ds(k, size)] * vector[1]
            + blocks[first + 3 * i + 2, pl.ds(k, size)] * vector[2]
            for i in range(3)
        ]

    SC = 2

    def invert(j, _):
        k = 1 + j * SC
        sums, faces = across_of(1, k, SC)
        m = [fine[i, pl.ds(k, SC)] for i in range(9)]
        b = [fine[9 + i, pl.ds(k, SC)] + faces * m[i] for i in range(9)]
        p = total[pl.ds(k + 6, SC)]
        where = planes(base - 5 + k, SC)
        inside = (where >= start - 2) & (where < end + 2) & (where >= 0) & (where < grid)
        goal = [
            jnp.where(inside, fine[18 + i, pl.ds(k, SC)] - b[3 * i] * p + sums[i], 0.0)
            for i in range(3)
        ]
        for i in range(3):
            target[i, pl.ds(k, SC)] = goal[i]
        cofactor = [
            b[4] * b[8] - b[5] * b[7],
            b[2] * b[7] - b[1] * b[8],
            b[1] * b[5] - b[2] * b[4],
            b[5] * b[6] - b[3] * b[8],
            b[0] * b[8] - b[2] * b[6],
            b[2] * b[3] - b[0] * b[5],
            b[3] * b[7] - b[4] * b[6],
            b[1] * b[6] - b[0] * b[7],
            b[0] * b[4] - b[1] * b[3],
        ]
        det = b[0] * cofactor[0] + b[1] * cofactor[3] + b[2] * cofactor[6]
        scale = 1.0 / jnp.where(inside, det, 1.0)
        inv = [jnp.where(inside, value * scale, 0.0) for value in cofactor]
        for i in range(3):
            value = 0.0
            for c in range(3):
                blocks[3 * i + c, pl.ds(k, SC)] = inv[3 * i + c]
                g = m[3 * i] * inv[c] + m[3 * i + 1] * inv[3 + c] + m[3 * i + 2] * inv[6 + c]
                blocks[9 + 3 * i + c, pl.ds(k, SC)] = g
                value = value + g * goal[c]
            carried[0, i, pl.ds(k, SC)] = value
        return 0

    lax.fori_loop(0, SW // SC, invert, 0)
    for i in range(3):
        carried[1, i, 0:1] = zero
        carried[1, i, FW - 1 : FW] = zero

    for sweep in range(SWEEPS - 1):
        now, later = sweep % 2, (sweep + 1) % 2

        def relax(j, _, now=now, later=later, last=sweep == SWEEPS - 2):
            k = 1 + j * SC
            sums, _ = across_of(now, k, SC)
            vector = [target[i, pl.ds(k, SC)] + sums[i] for i in range(3)]
            new = times(0 if last else 9, k, SC, vector)
            if last:
                new[0] = new[0] + total[pl.ds(k + 6, SC)]
            for i in range(3):
                if last:
                    result[i, pl.ds(k, SC)] = new[i]
                else:
                    carried[later, i, pl.ds(k, SC)] = new[i]
            return 0

        lax.fori_loop(0, SW // SC, relax, 0)

    slot_ids = planes(0, CAP)
    for i in range(3):
        value = result[i, pl.ds(drift + 5, CAP)]
        out[i] = jnp.where(slot_ids < count, value, 0.0)

    for step, copy in copies:

        @pl.when(here[step])
        def _():
            copy.wait_send()


def on_device(counts, resid, accum, mobility, trans, decouple):
    n = lax.axis_size("gx")
    f32 = jnp.float32

    def vmem(*dims):
        return pltpu.VMEM(dims + (8, 128), f32)

    value = pl.pallas_call(
        functools.partial(kernel, n),
        out_shape=jax.ShapeDtypeStruct((3, CAP, 8, 128), f32),
        in_specs=[pl.BlockSpec(memory_space=pltpu.SMEM)]
        + [pl.BlockSpec(memory_space=pltpu.VMEM)] * 5,
        out_specs=pl.BlockSpec(memory_space=pltpu.VMEM),
        scratch_shapes=[
            vmem(26, OWN),
            vmem(6, 12),
            vmem(6, 12),
            vmem(6, 12),
            vmem(6, 5),
            vmem(6, 5),
            vmem(21, 3),
            vmem(21, HALO),
            vmem(21, HALO),
            vmem(6, PW),
            vmem(6, PW),
            vmem(2, PW),
            vmem(PW),
            vmem(PW),
            vmem(21, FW),
            vmem(18, FW),
            vmem(2, 3, FW),
            vmem(3, FW),
            vmem(3, 24),
            pltpu.SemaphoreType.DMA((6,)),
            pltpu.SemaphoreType.DMA((6,)),
        ],
        compiler_params=pltpu.CompilerParams(
            collective_id=0, has_side_effects=True, vmem_limit_bytes=40 * 1024 * 1024
        ),
    )(counts, resid, accum, mobility, trans, decouple)
    return value.reshape(3, CAP, 1024)


def solution(mesh):
    spec = P(None, ("groups", "gx"), None)
    return jax.shard_map(
        on_device,
        mesh=mesh,
        in_specs=(P("groups"),) + (spec,) * 5,
        out_specs=spec,
        check_vma=False,
    )
```

time: 135 us -> 35.7 us (0.26)
  the two profiles are of different devices: /device:TPU:5 before, /device:TPU:16 now
where the time goes in v1:
time: 35.7 us; the launch traced here: 35.4 us
  Pallas kernels  29.2 us (82%)
  local copies, waits for them, and re-layouts  6.25 us (18%)
    pallas_call x1, Pallas kernels, on_device(): pl.pallas_call(functools.partial(kernel, n), out_shape=jax.ShapeDtypeStru...  29.2 us
    unnamed x12, local copies, waits for them, and re-layouts  5.54 us

profile of v1, /device:TPU:16, one launch (start us, length us, event | category | flops | bytes accessed | tf_op | source)
XLA Modules:
  0.0 35.4 jit_solution(9905121645640102140)
XLA Ops:
  0.0 0.0 copy-start
  0.0 1.1 %copy-done = f32[9,16,1024]{2,1,0:T(8,128)S(1)} copy-done((f32[9,16,1024]{2,1,0:T(8,128)S(1)}, f32[9,16,1024]{2,1,0:T(8,128)}, u32[]{:S(2)}) %copy-start) | copy-done | bytes 589848
  1.1 0.0 copy-start.1
  1.1 1.1 %copy-done.1 = f32[9,16,1024]{2,1,0:T(8,128)S(1)} copy-done((f32[9,16,1024]{2,1,0:T(8,128)S(1)}, f32[9,16,1024]{2,1,0:T(8,128)}, u32[]{:S(2)}) %copy-start.1) | copy-done | bytes 589848
  2.1 0.0 copy-start.2
  2.1 0.9 %copy-done.2 = f32[3,16,1024]{2,1,0:T(8,128)S(1)} copy-done((f32[3,16,1024]{2,1,0:T(8,128)S(1)}, f32[3,16,1024]{2,1,0:T(8,128)}, u32[]{:S(2)}) %copy-start.2) | copy-done | bytes 196632
  3.1 0.0 copy-start.3
  3.1 0.9 %copy-done.3 = f32[3,16,1024]{2,1,0:T(8,128)S(1)} copy-done((f32[3,16,1024]{2,1,0:T(8,128)S(1)}, f32[3,16,1024]{2,1,0:T(8,128)}, u32[]{:S(2)}) %copy-start.3) | copy-done | bytes 196632
  4.0 0.0 copy-start.4
  4.0 0.9 %copy-done.4 = f32[2,16,1024]{2,1,0:T(8,128)S(1)} copy-done((f32[2,16,1024]{2,1,0:T(8,128)S(1)}, f32[2,16,1024]{2,1,0:T(8,128)}, u32[]{:S(2)}) %copy-start.4) | copy-done | bytes 131096
  4.9 0.0 copy-start.5
  4.9 0.7 %copy-done.5 = s32[16]{0:T(128)S(1)} copy-done((s32[16]{0:T(128)S(1)}, s32[16]{0:T(128)}, u32[]{:S(2)}) %copy-start.5) | copy-done | bytes 88
  5.5 29.2 %shard_map.64 = f32[3,16,8,128]{3,2,1,0:T(8,128)S(1)} custom-call(s32[16]{0:T(128)S(1)} %copy-done.5, f32[3,16,1024]{2,1,0:T(8,128)S(1)} %copy-done.2, f32[9,16,1024]{2,1,0:T(8,128)S(1)} %copy-done, f32[9,16,1024]{2,1,0:T(8,128)S(1)} %copy-done.1, f32[3,16,1024]{2,1,0:T(8,128)S(1)} %copy-done.3, f32[2,16,1024]{2,1,0:T(8,128)S(1)} %copy-done.4), custom_call_target="tpu_custom_call" | custom-call | tf_op jit(solution)/shard_map/pallas_call | solution.py:393
  34.7 0.7 %reshape.3 = f32[3,16,1024]{2,1,0:T(8,128)} reshape(f32[3,16,8,128]{3,2,1,0:T(8,128)S(1)} %shard_map.64) | data formatting | bytes 393216 | tf_op jit(solution)/shard_map/reshape | solution.py:426
Async XLA Ops:
  0.0 1.1 %copy-start = (f32[9,16,1024]{2,1,0:T(8,128)S(1)}, f32[9,16,1024]{2,1,0:T(8,128)}, u32[]{:S(2)}) copy-start(f32[9,16,1024]{2,1,0:T(8,128)} %accum.1) | copy-start | bytes 1769476
  1.1 1.1 %copy-start.1 = (f32[9,16,1024]{2,1,0:T(8,128)S(1)}, f32[9,16,1024]{2,1,0:T(8,128)}, u32[]{:S(2)}) copy-start(f32[9,16,1024]{2,1,0:T(8,128)} %mobility.1) | copy-start | bytes 1769476
  2.1 0.9 %copy-start.2 = (f32[3,16,1024]{2,1,0:T(8,128)S(1)}, f32[3,16,1024]{2,1,0:T(8,128)}, u32[]{:S(2)}) copy-start(f32[3,16,1024]{2,1,0:T(8,128)} %resid.1) | copy-start | bytes 589828
  3.1 0.9 %copy-start.3 = (f32[3,16,1024]{2,1,0:T(8,128)S(1)}, f32[3,16,1024]{2,1,0:T(8,128)}, u32[]{:S(2)}) copy-start(f32[3,16,1024]{2,1,0:T(8,128)} %trans.1) | copy-start | bytes 589828
  4.0 0.9 %copy-start.4 = (f32[2,16,1024]{2,1,0:T(8,128)S(1)}, f32[2,16,1024]{2,1,0:T(8,128)}, u32[]{:S(2)}) copy-start(f32[2,16,1024]{2,1,0:T(8,128)} %decouple.1) | copy-start | bytes 393220
  4.9 0.7 %copy-start.5 = (s32[16]{0:T(128)S(1)}, s32[16]{0:T(128)}, u32[]{:S(2)}) copy-start(s32[16]{0:T(128)} %counts.1) | copy-start | bytes 196

commit v2 on v1

--- a/solution.py
+++ b/solution.py
@@ -43,13 +43,19 @@
 
 def kernel(
     n,
+    counts_hbm,
+    resid_hbm,
+    accum_hbm,
+    mobility_hbm,
+    trans_hbm,
+    decouple_hbm,
+    out,
     counts,
     resid,
     accum,
     mobility,
     trans,
     decouple,
-    out,
     own,
     pown,
     below1,
@@ -71,8 +77,22 @@
     result,
     send_sem,
     recv_sem,
+    load_sem,
 ):
     me = lax.axis_index("gx")
+    pairs = [
+        (counts_hbm, counts),
+        (mobility_hbm, mobility),
+        (accum_hbm, accum),
+        (resid_hbm, resid),
+        (trans_hbm, trans),
+        (decouple_hbm, decouple),
+    ]
+    loads = [
+        pltpu.make_async_copy(src, dst, load_sem.at[i]) for i, (src, dst) in enumerate(pairs)
+    ]
+    for load in loads:
+        load.start()
     grid = CX * n
     barrier = pltpu.get_barrier_semaphore()
     here = {}
@@ -85,6 +105,7 @@
                 barrier, inc=1, device_id={"gx": me + step}, device_id_type=pl.DeviceIdType.MESH
             )
 
+    loads[0].wait()
     start = jnp.int32(0)
     for part in range(n):
         start = start + jnp.where(part < me, counts[part], 0)
@@ -104,18 +125,22 @@
         return first + lax.broadcasted_iota(jnp.int32, (length, 8, 128), 0)
 
     blank = jnp.zeros((LEAD, 8, 128), jnp.float32)
-    order = [(mobility, i) for i in range(9)] + [(accum, i) for i in range(9)]
-    order += [(resid, i) for i in range(3)] + [(trans, i) for i in range(3)]
-    order += [(decouple, i) for i in range(2)]
-    spans = [(mobility, 0, 9), (accum, 9, 9), (resid, 18, 3), (trans, 21, 3), (decouple, 24, 2)]
-    for ref, first, length in spans:
-
-        def place(i, _, ref=ref, first=first):
-            own[first + i, :LEAD] = blank
-            own[first + i, LEAD:] = ref[i].reshape(CAP, 8, 128)
-            return 0
-
-        lax.fori_loop(0, length, place, 0)
+    columns = (0, 3, 6, 1, 2, 4, 5, 7, 8)
+    place_of = {c: i for i, c in enumerate(columns)}
+
+    def place(i, ref, at):
+        own[i, :LEAD] = blank
+        own[i, LEAD:] = ref[at].reshape(CAP, 8, 128)
+
+    for load in loads[1:]:
+        load.wait()
+    for i in range(3):
+        place(i, mobility, 3 * i)
+        place(9 + 3 * i, accum, 3 * i)
+        place(18 + i, resid, i)
+        place(21 + i, trans, i)
+    for i in range(2):
+        place(24 + i, decouple, i)
 
     at = 5 - drift
     spot = planes(base - 2, 12)
@@ -126,14 +151,11 @@
 
     one, two = field(24), field(25)
     pown[0] = jnp.where(mine, field(18) + one * field(19) + two * field(20), 0.0)
-    pown[1] = jnp.where(mine, field(0) + one * field(3) + two * field(6), 0.0)
+    pown[1] = jnp.where(mine, field(0) + one * field(1) + two * field(2), 0.0)
     pown[2] = jnp.where(mine, field(9) + one * field(12) + two * field(15), 0.0)
     pown[3] = jnp.where(mine & (spot < grid - 1), field(21), 0.0)
     pown[4] = jnp.where(mine, field(22) * keep_row, 0.0)
     pown[5] = jnp.where(mine, field(23) * keep_lane, 0.0)
-
-    for i in range(21):
-        fup[i] = own[i, pl.ds(LEAD + jnp.clip(count, 4, 12) - 3, 3)]
 
     for step, ref in ((-1, below1), (1, above1), (-2, below2), (2, above2)):
 
@@ -161,14 +183,27 @@
         (-1, send(pown, above1, -1, 1)),
         (2, send(pown.at[:, 7:12], below2, 2, 2)),
         (-2, send(pown.at[:, 0:5], above2, -2, 3)),
-        (1, send(fup, fbelow.at[:, 4:7], 1, 4)),
-        (-1, send(own.at[0:21, LEAD : LEAD + 3], fabove.at[:, 4:7], -1, 5)),
+        (1, send(fup.at[0:3], fbelow.at[0:3, 4:7], 1, 4)),
+        (1, send(fup.at[3:21, 1:3], fbelow.at[3:21, 5:7], 1, 5)),
+        (-1, send(own.at[0:3, LEAD : LEAD + 3], fabove.at[0:3, 4:7], -1, 6)),
+        (-1, send(own.at[3:21, LEAD : LEAD + 2], fabove.at[3:21, 4:6], -1, 7)),
     ]
-    for step, copy in copies:
-
-        @pl.when(here[step])
-        def _():
-            copy.start()
+
+    def start_all(some):
+        for step, copy in some:
+
+            @pl.when(here[step])
+            def _():
+                copy.start()
+
+    start_all(copies[:4])
+    for i in range(3):
+        for c in (1, 2):
+            place(place_of[3 * i + c], mobility, 3 * i + c)
+            place(9 + 3 * i + c, accum, 3 * i + c)
+    for i in range(21):
+        fup[i] = own[i, pl.ds(LEAD + jnp.clip(count, 4, 12) - 3, 3)]
+    start_all(copies[4:])
 
     for step, copy in copies[:4]:
 
@@ -263,24 +298,25 @@
         return (spot >= start) & (spot < end)
 
     low_mine, mid_mine, high_mine = owned(spot_low), owned(spot_mid), owned(spot_high)
-    low_near = (spot_low >= start - 3) & (spot_low < start) & (spot_low >= 0)
-    high_near = (spot_high >= end) & (spot_high < end + 3) & (spot_high < grid)
-
-    def assemble(i, _):
-        low = jnp.where(low_near, fbelow[i, pl.ds(at_below, 7)], 0.0)
-        high = jnp.where(high_near, fabove[i, pl.ds(at_above, 7)], 0.0)
-        fine[i, 0:7] = jnp.where(low_mine, own[i, pl.ds(at_own, 7)], low)
-        fine[i, 7:11] = jnp.where(mid_mine, own[i, pl.ds(at_own + 7, 4)], 0.0)
-        fine[i, 11:18] = jnp.where(high_mine, own[i, pl.ds(at_own + 11, 7)], high)
-        return 0
-
-    lax.fori_loop(0, 21, assemble, 0)
+    for first, last, width in ((0, 3, 3), (3, 21, 2)):
+        low_near = (spot_low >= start - width) & (spot_low < start) & (spot_low >= 0)
+        high_near = (spot_high >= end) & (spot_high < end + width) & (spot_high < grid)
+
+        def assemble(i, _, low_near=low_near, high_near=high_near):
+            low = jnp.where(low_near, fbelow[i, pl.ds(at_below, 7)], 0.0)
+            high = jnp.where(high_near, fabove[i, pl.ds(at_above, 7)], 0.0)
+            fine[i, 0:7] = jnp.where(low_mine, own[i, pl.ds(at_own, 7)], low)
+            fine[i, 7:11] = jnp.where(mid_mine, own[i, pl.ds(at_own + 7, 4)], 0.0)
+            fine[i, 11:18] = jnp.where(high_mine, own[i, pl.ds(at_own + 11, 7)], high)
+            return 0
+
+        lax.fori_loop(first, last, assemble, 0)
 
     for i in range(3):
         for slot in range(2):
             carried[slot, i, 0:1] = zero
             carried[slot, i, FW - 1 : FW] = zero
-        carried[1, i] = fine[3 * i] * total[6 : 6 + FW]
+        carried[1, i] = fine[i] * total[6 : 6 + FW]
 
     def across_of(slot, k, size):
         tx = pw[3, pl.ds(k + 6, size)]
@@ -312,7 +348,7 @@
     def invert(j, _):
         k = 1 + j * SC
         sums, faces = across_of(1, k, SC)
-        m = [fine[i, pl.ds(k, SC)] for i in range(9)]
+        m = [fine[place_of[i], pl.ds(k, SC)] for i in range(9)]
         b = [fine[9 + i, pl.ds(k, SC)] + faces * m[i] for i in range(9)]
         p = total[pl.ds(k + 6, SC)]
         where = planes(base - 5 + k, SC)
@@ -393,10 +429,15 @@
     value = pl.pallas_call(
         functools.partial(kernel, n),
         out_shape=jax.ShapeDtypeStruct((3, CAP, 8, 128), f32),
-        in_specs=[pl.BlockSpec(memory_space=pltpu.SMEM)]
-        + [pl.BlockSpec(memory_space=pltpu.VMEM)] * 5,
+        in_specs=[pl.BlockSpec(memory_space=pltpu.HBM)] * 6,
         out_specs=pl.BlockSpec(memory_space=pltpu.VMEM),
         scratch_shapes=[
+            pltpu.SMEM((n,), jnp.int32),
+            pltpu.VMEM((3, CAP, 1024), f32),
+            pltpu.VMEM((9, CAP, 1024), f32),
+            pltpu.VMEM((9, CAP, 1024), f32),
+            pltpu.VMEM((3, CAP, 1024), f32),
+            pltpu.VMEM((2, CAP, 1024), f32),
             vmem(26, OWN),
             vmem(6, 12),
             vmem(6, 12),
@@ -416,11 +457,12 @@
             vmem(2, 3, FW),
             vmem(3, FW),
             vmem(3, 24),
-            pltpu.SemaphoreType.DMA((6,)),
+            pltpu.SemaphoreType.DMA((8,)),
+            pltpu.SemaphoreType.DMA((8,)),
             pltpu.SemaphoreType.DMA((6,)),
         ],
         compiler_params=pltpu.CompilerParams(
-            collective_id=0, has_side_effects=True, vmem_limit_bytes=40 * 1024 * 1024
+            collective_id=0, has_side_effects=True, vmem_limit_bytes=64 * 1024 * 1024
         ),
     )(counts, resid, accum, mobility, trans, decouple)
     return value.reshape(3, CAP, 1024)

time: 35.7 us -> 30.3 us (0.85)
  the two profiles are of different devices: /device:TPU:16 before, /device:TPU:10 now
where the time goes in v2:
time: 30.3 us; the launch traced here: 30.2 us
  Pallas kernels  28.5 us (94%)
  local copies, waits for them, and re-layouts  1.64 us (5%)
    pallas_call x1, Pallas kernels, on_device(): pl.pallas_call(functools.partial(kernel, n), out_shape=jax.ShapeDtypeStru...  28.5 us
    reshape x1, local copies, waits for them, and re-layouts, on_device(): return value.reshape(3, CAP, 1024)  1.64 us

profile of v2, /device:TPU:10, one launch (start us, length us, event | category | flops | bytes accessed | tf_op | source)
XLA Modules:
  0.0 30.2 jit_solution(10202537513530166635)
XLA Ops:
  0.0 28.5 %shard_map.64 = f32[3,16,8,128]{3,2,1,0:T(8,128)} custom-call(s32[16]{0:T(128)} %counts_hbm.1, f32[3,16,1024]{2,1,0:T(8,128)} %resid_hbm.1, f32[9,16,1024]{2,1,0:T(8,128)} %accum_hbm.1, f32[9,16,1024]{2,1,0:T(8,128)} %mobility_hbm.1, f32[3,16,1024]{2,1,0:T(8,128)} %trans_hbm.1, f32[2,16,1024]{2,1,0:T(8,128)} %decouple_hbm.1), custom_call_target="tpu_custom_call" | custom-call | tf_op jit(solution)/shard_map/pallas_call | solution.py:429
  28.5 1.6 %reshape.3 = f32[3,16,1024]{2,1,0:T(8,128)} reshape(f32[3,16,8,128]{3,2,1,0:T(8,128)} %shard_map.64) | data formatting | bytes 393216 | tf_op jit(solution)/shard_map/reshape | solution.py:468

commit v3 on v2

--- a/solution.py
+++ b/solution.py
@@ -229,7 +229,7 @@
     middle = 0.5 * (CHEB_HIGH + CHEB_LOW)
     radius = 0.5 * (CHEB_HIGH - CHEB_LOW)
     aspect = middle / radius
-    PC = 4
+    PC = 28
 
     def prepare(j, _):
         k = 1 + j * PC
@@ -343,7 +343,7 @@
             for i in range(3)
         ]
 
-    SC = 2
+    SC = 16
 
     def invert(j, _):
         k = 1 + j * SC

time: 30.3 us -> 24.5 us (0.81)
  the two profiles are of different devices: /device:TPU:10 before, /device:TPU:11 now
where the time goes in v3:
time: 24.5 us; the launch traced here: 24.4 us
  Pallas kernels  22.7 us (93%)
  local copies, waits for them, and re-layouts  1.64 us (7%)
    pallas_call x1, Pallas kernels, on_device(): pl.pallas_call(functools.partial(kernel, n), out_shape=jax.ShapeDtypeStru...  22.7 us
    reshape x1, local copies, waits for them, and re-layouts, on_device(): return value.reshape(3, CAP, 1024)  1.64 us

profile of v3, /device:TPU:11, one launch (start us, length us, event | category | flops | bytes accessed | tf_op | source)
XLA Modules:
  0.0 24.4 jit_solution(1767265220844543652)
XLA Ops:
  0.0 22.7 %shard_map.64 = f32[3,16,8,128]{3,2,1,0:T(8,128)} custom-call(s32[16]{0:T(128)} %counts_hbm.1, f32[3,16,1024]{2,1,0:T(8,128)} %resid_hbm.1, f32[9,16,1024]{2,1,0:T(8,128)} %accum_hbm.1, f32[9,16,1024]{2,1,0:T(8,128)} %mobility_hbm.1, f32[3,16,1024]{2,1,0:T(8,128)} %trans_hbm.1, f32[2,16,1024]{2,1,0:T(8,128)} %decouple_hbm.1), custom_call_target="tpu_custom_call" | custom-call | tf_op jit(solution)/shard_map/pallas_call | solution.py:429
  22.7 1.6 %reshape.3 = f32[3,16,1024]{2,1,0:T(8,128)} reshape(f32[3,16,8,128]{3,2,1,0:T(8,128)} %shard_map.64) | data formatting | bytes 393216 | tf_op jit(solution)/shard_map/reshape | solution.py:468

commit v4 on v3

v4 whole, which is shorter than its diff:
```python
import functools

import jax
import jax.numpy as jnp
from jax import lax
from jax.experimental import pallas as pl
from jax.experimental.pallas import tpu as pltpu
from jax.sharding import PartitionSpec as P

CX = 8
NZ = 32
CHEB = 6
SWEEPS = 6
CAP = 16
CHEB_LOW = 0.1
CHEB_HIGH = 2.0

LEAD = 8
OWN = LEAD + CAP
PW = 20
SW = 16
OW = 12


def y_next(x, lane):
    r = pltpu.roll(x, 96, x.ndim - 1)
    return jnp.where(lane < 96, r, pltpu.roll(r, 7, x.ndim - 2))


def y_prev(x, lane):
    r = pltpu.roll(x, 32, x.ndim - 1)
    return jnp.where(lane >= 32, r, pltpu.roll(r, 1, x.ndim - 2))


def z_next(x):
    return pltpu.roll(x, 127, x.ndim - 1)


def z_prev(x):
    return pltpu.roll(x, 1, x.ndim - 1)


def kernel(
    n,
    counts_hbm,
    resid_hbm,
    accum_hbm,
    mobility_hbm,
    trans_hbm,
    decouple_hbm,
    out,
    counts,
    resid,
    accum,
    mobility,
    trans,
    decouple,
    own,
    pslot,
    pup,
    pbelow,
    pabove,
    pw,
    coef,
    state,
    bup,
    bdown,
    bbelow,
    babove,
    column,
    inverse,
    gain,
    gup,
    gdown,
    gbelow,
    gabove,
    carried,
    target,
    rup,
    rdown,
    rbelow,
    rabove,
    result,
    send_sem,
    recv_sem,
    load_sem,
):
    me = lax.axis_index("gx")
    pairs = [
        (counts_hbm, counts),
        (mobility_hbm, mobility),
        (accum_hbm, accum),
        (resid_hbm, resid),
        (trans_hbm, trans),
        (decouple_hbm, decouple),
    ]
    loads = [
        pltpu.make_async_copy(src, dst, load_sem.at[i]) for i, (src, dst) in enumerate(pairs)
    ]
    for load in loads:
        load.start()
    barrier = pltpu.get_barrier_semaphore()
    here = {-1: me > 0, 1: me < n - 1}
    for step in here:

        @pl.when(here[step])
        def _():
            pl.semaphore_signal(
                barrier, inc=1, device_id={"gx": me + step}, device_id_type=pl.DeviceIdType.MESH
            )

    loads[0].wait()
    start = jnp.int32(0)
    for part in range(n):
        start = start + jnp.where(part < me, counts[part], 0)
    count = counts[me]
    end = start + count
    base = CX * me
    drift = jnp.clip(start - base, -2, 2)
    drift_end = jnp.clip(end - base - CX, -2, 2)
    tail = jnp.clip(count, 4, 12)
    low_at = 2 - drift
    high_at = 2 - drift_end

    shape = (1, 8, 128)
    lane = lax.broadcasted_iota(jnp.int32, shape, 2)
    row = lax.broadcasted_iota(jnp.int32, shape, 1)
    keep_row = jnp.where((row < 7) | (lane < 96), 1.0, 0.0)
    keep_lane = jnp.where(lane % NZ < NZ - 1, 1.0, 0.0)

    def planes(first, length):
        return first + lax.broadcasted_iota(jnp.int32, (length, 8, 128), 0)

    def tiles(value):
        return value.reshape(CAP, 8, 128)

    blank = jnp.zeros((LEAD, 8, 128), jnp.float32)
    zero = jnp.zeros((1, 8, 128), jnp.float32)
    slot_ids = planes(0, CAP)
    held = slot_ids < count

    for load in loads[1:]:
        load.wait()
    one, two = decouple[0], decouple[1]
    fields = [
        tiles(mobility[0] + one * mobility[3] + two * mobility[6]),
        jnp.where(slot_ids + start < CX * n - 1, tiles(trans[0]), 0.0),
        tiles(resid[0] + one * resid[1] + two * resid[2]),
        tiles(accum[0] + one * accum[3] + two * accum[6]),
        tiles(trans[1]) * keep_row,
        tiles(trans[2]) * keep_lane,
        tiles(mobility[0]),
        tiles(mobility[3]),
        tiles(mobility[6]),
    ]
    for i, value in enumerate(fields):
        pslot[i, :LEAD] = blank
        pslot[i, LEAD:] = jnp.where(held, value, 0.0)
    for i in range(9):
        pup[i] = pslot[i, pl.ds(LEAD + tail - 4, 4)]

    pl.semaphore_wait(barrier, here[-1].astype(jnp.int32) + here[1].astype(jnp.int32))

    def send(src, dst, step, slot):
        return pltpu.make_async_remote_copy(
            src_ref=src,
            dst_ref=dst,
            send_sem=send_sem.at[slot],
            recv_sem=recv_sem.at[slot],
            device_id={"gx": me + step},
            device_id_type=pl.DeviceIdType.MESH,
        )

    L = LEAD
    phase_a = [
        (1, send(pup.at[0:2], pbelow.at[0:2, 4:8], 1, 0)),
        (-1, send(pslot.at[0:2, L : L + 4], pabove.at[0:2, 4:8], -1, 1)),
        (1, send(pup.at[2:6, 1:4], pbelow.at[2:6, 5:8], 1, 2)),
        (-1, send(pslot.at[2:6, L : L + 3], pabove.at[2:6, 4:7], -1, 3)),
    ]
    phase_m = [
        (1, send(pup.at[6:9, 3:4], pbelow.at[6:9, 7:8], 1, 4)),
        (-1, send(pslot.at[6:9, L : L + 1], pabove.at[6:9, 4:5], -1, 5)),
    ]
    phase_b = [
        (1, send(bup, bbelow.at[:, 4:7], 1, 6)),
        (-1, send(bdown, babove.at[:, 4:7], -1, 7)),
    ]
    phase_g = [
        (1, send(gup, gbelow.at[:, 4:6], 1, 8)),
        (-1, send(gdown, gabove.at[:, 4:6], -1, 9)),
    ]
    phase_r = [
        (1, send(rup, rbelow.at[:, 4:6], 1, 10)),
        (-1, send(rdown, rabove.at[:, 4:6], -1, 11)),
    ]

    def begin(phase):
        for step, copy in phase:

            @pl.when(here[step])
            def _(copy=copy):
                copy.start()

    def arrive(phase):
        for step, copy in phase:

            @pl.when(here[-step])
            def _(copy=copy):
                copy.wait_recv()

    begin(phase_a)
    begin(phase_m)

    rest = [(mobility, 3 * i + c) for i in range(3) for c in (1, 2)]
    rest += [(accum, i) for i in range(9)] + [(resid, i) for i in range(3)]
    for i, (ref, at) in enumerate(rest):
        own[i, :LEAD] = blank
        own[i, LEAD:] = tiles(ref[at])

    arrive(phase_a)
    arrive(phase_m)

    spot_low, spot_high = planes(base - 6, 8), planes(base + 6, 8)

    def near_low(width):
        return (spot_low >= start - width) & (spot_low < start) & (spot_low >= 0)

    def near_high(width):
        return (spot_high >= end) & (spot_high < end + width) & (spot_high < CX * n)

    for i in range(9):
        width = 4 if i < 2 else 3 if i < 6 else 1
        mine = pslot[i, pl.ds(low_at, PW)]
        pw[i, 0:8] = jnp.where(near_low(width), pbelow[i, pl.ds(low_at, 8)], mine[0:8])
        pw[i, 8:12] = mine[8:12]
        pw[i, 12:20] = jnp.where(near_high(width), pabove[i, pl.ds(high_at, 8)], mine[12:20])

    middle = 0.5 * (CHEB_HIGH + CHEB_LOW)
    radius = 0.5 * (CHEB_HIGH - CHEB_LOW)
    aspect = middle / radius
    inner = slice(1, PW - 1)
    for i in range(2):
        state[i, 0:1] = zero
        state[i, PW - 1 : PW] = zero
    lam = pw[0]
    cx_all = pw[1, 0 : PW - 1] * (lam[0 : PW - 1] + lam[1:PW]) * 0.5
    cx, cx_down = cx_all[1:], cx_all[:-1]
    lam = lam[inner]
    cy = pw[4, inner] * (lam + y_next(lam, lane)) * 0.5
    cz = pw[5, inner] * (lam + z_next(lam)) * 0.5
    cy_down = y_prev(cy, lane)
    cz_down = z_prev(cz)
    pivot = pw[3, inner] + cx + cx_down + cy + cy_down + cz + cz_down
    spot = planes(base - 5, PW - 2)
    valid = (spot >= start - 3) & (spot < end + 3) & (spot >= 0) & (spot < CX * n)
    scale = 1.0 / jnp.where(valid, pivot, 1.0)
    for i, value in enumerate((cx, cx_down, cy, cy_down, cz, cz_down)):
        coef[i] = value * scale
    scaled = pw[2, inner] * scale
    state[2, inner] = scaled
    state[0, inner] = scaled / middle
    state[3, inner] = scaled / middle
    pw[9, inner] = y_prev(pw[4, inner], lane)
    pw[10, inner] = z_prev(pw[5, inner])

    def advance(iteration, factor):
        now, later = iteration % 2, (iteration + 1) % 2
        factor_next = 1.0 / (2.0 * aspect - factor)
        d = state[now, inner]
        across = coef[0] * state[now, 2:PW] + coef[1] * state[now, 0 : PW - 2]
        across = across + coef[2] * y_next(d, lane) + coef[3] * y_prev(d, lane)
        across = across + coef[4] * z_next(d) + coef[5] * z_prev(d)
        e = state[2, inner] - d + across
        state[2, inner] = e
        d = (factor_next * factor) * d + (2.0 * factor_next / radius) * e
        state[later, inner] = d
        state[3, inner] = state[3, inner] + d
        return factor_next

    factor = 1.0 / aspect
    for iteration in range(3):
        factor = advance(iteration, factor)

    for i in range(3):
        bup[i] = state[1 + i, pl.ds(11 + drift_end, 3)]
        bdown[i] = state[1 + i, pl.ds(6 + drift, 3)]
    begin(phase_b)

    spot = planes(base - 2, OW)
    mine = (spot >= start) & (spot < end)
    middle_planes = slice(4, 4 + OW)
    faces = pw[1, middle_planes] + pw[1, 3 : 3 + OW] + pw[4, middle_planes] + pw[9, middle_planes]
    faces = faces + pw[5, middle_planes] + pw[10, middle_planes]

    def block(i):
        return own[i, pl.ds(low_at + 4, OW)]

    m = []
    for i in range(3):
        m += [pw[6 + i, middle_planes], block(2 * i), block(2 * i + 1)]
    b = [block(6 + i) + faces * m[i] for i in range(9)]
    cofactor = [
        b[4] * b[8] - b[5] * b[7],
        b[2] * b[7] - b[1] * b[8],
        b[1] * b[5] - b[2] * b[4],
        b[5] * b[6] - b[3] * b[8],
        b[0] * b[8] - b[2] * b[6],
        b[2] * b[3] - b[0] * b[5],
        b[3] * b[7] - b[4] * b[6],
        b[1] * b[6] - b[0] * b[7],
        b[0] * b[4] - b[1] * b[3],
    ]
    det = b[0] * cofactor[0] + b[1] * cofactor[3] + b[2] * cofactor[6]
    scale = 1.0 / jnp.where(mine, det, 1.0)
    inv = [jnp.where(mine, value * scale, 0.0) for value in cofactor]
    edge = jnp.zeros((2, 8, 128), jnp.float32)
    for i in range(3):
        column[i] = b[3 * i]
        for c in range(3):
            inverse[3 * i + c] = inv[3 * i + c]
            value = m[3 * i] * inv[c] + m[3 * i + 1] * inv[3 + c] + m[3 * i + 2] * inv[6 + c]
            gain[3 * i + c, 0:2] = edge
            gain[3 * i + c, 2 : 2 + OW] = jnp.where(mine, value, 0.0)
            gain[3 * i + c, 2 + OW : SW] = edge
    for i in range(9):
        gup[i] = gain[i, pl.ds(10 + drift_end, 2)]
        gdown[i] = gain[i, pl.ds(4 + drift, 2)]
    begin(phase_g)

    arrive(phase_b)
    for i in range(3):
        low = jnp.where(near_low(3)[1:8], bbelow[i, pl.ds(low_at, 7)], state[1 + i, 1:8])
        high = jnp.where(near_high(3)[0:7], babove[i, pl.ds(high_at, 7)], state[1 + i, 12:19])
        state[1 + i, 1:8] = low
        state[1 + i, 12:19] = high
    for iteration in range(3, CHEB - 1):
        factor = advance(iteration, factor)

    for i in range(3):
        for slot in range(2):
            carried[slot, i, 0:1] = zero
            carried[slot, i, SW + 1 : SW + 2] = zero

    def across_of(first, u, up, down, length):
        here_planes = slice(first, first + length)
        value = pw[1, here_planes] * up + pw[1, first - 1 : first - 1 + length] * down
        value = value + pw[4, here_planes] * y_next(u, lane) + pw[9, here_planes] * y_prev(u, lane)
        return value + pw[5, here_planes] * z_next(u) + pw[10, here_planes] * z_prev(u)

    pressure = state[3, 3 : 5 + OW]
    for i in range(3):
        v = pw[6 + i, 3 : 5 + OW] * pressure
        sums = across_of(4, v[1 : 1 + OW], v[2 : 2 + OW], v[0:OW], OW)
        goal = own[15 + i, pl.ds(low_at + 4, OW)] - column[i] * pressure[1 : 1 + OW] + sums
        target[i, 0:2] = edge
        target[i, 2 : 2 + OW] = jnp.where(mine, goal, 0.0)
        target[i, 2 + OW : SW] = edge
    for i in range(3):
        rup[i] = target[i, pl.ds(10 + drift_end, 2)]
        rdown[i] = target[i, pl.ds(4 + drift, 2)]
    begin(phase_r)

    def merge(ref, i, below, above):
        low = jnp.where(near_low(2)[2:8], below[i, pl.ds(low_at, 6)], ref[i, 0:6])
        high = jnp.where(near_high(2)[0:6], above[i, pl.ds(high_at, 6)], ref[i, 10:16])
        ref[i, 0:6] = low
        ref[i, 10:16] = high

    arrive(phase_g)
    for i in range(9):
        merge(gain, i, gbelow, gabove)
    arrive(phase_r)
    for i in range(3):
        merge(target, i, rbelow, rabove)

    def times(blocks, vector):
        return [
            blocks[3 * i] * vector[0]
            + blocks[3 * i + 1] * vector[1]
            + blocks[3 * i + 2] * vector[2]
            for i in range(3)
        ]

    first = times(gain, [target[i] for i in range(3)])
    for i in range(3):
        carried[0, i, 1 : 1 + SW] = first[i]
    for sweep in range(SWEEPS - 2):
        now, later = sweep % 2, (sweep + 1) % 2
        vector = []
        for i in range(3):
            u = carried[now, i]
            sums = across_of(2, u[1 : 1 + SW], u[2 : 2 + SW], u[0:SW], SW)
            vector.append(target[i] + sums)
        new = times(gain, vector)
        for i in range(3):
            carried[later, i, 1 : 1 + SW] = new[i]
    now = (SWEEPS - 2) % 2
    vector = []
    for i in range(3):
        u = carried[now, i, 2 : 4 + OW]
        sums = across_of(4, u[1 : 1 + OW], u[2 : 2 + OW], u[0:OW], OW)
        vector.append(target[i, 2 : 2 + OW] + sums)
    new = times(inverse, vector)
    new[0] = new[0] + state[3, 4 : 4 + OW]
    for i in range(3):
        result[i, 0:OW] = new[i]
        value = result[i, pl.ds(2 + drift, CAP)]
        out[i] = jnp.where(held, value, 0.0)

    for step, copy in phase_a + phase_m + phase_b + phase_g + phase_r:

        @pl.when(here[step])
        def _(copy=copy):
            copy.wait_send()


def on_device(counts, resid, accum, mobility, trans, decouple):
    n = lax.axis_size("gx")
    f32 = jnp.float32

    def vmem(*dims):
        return pltpu.VMEM(dims + (8, 128), f32)

    raw = [pltpu.VMEM((fields, CAP, 1024), f32) for fields in (3, 9, 9, 3, 2)]
    value = pl.pallas_call(
        functools.partial(kernel, n),
        out_shape=jax.ShapeDtypeStruct((3, CAP, 8, 128), f32),
        in_specs=[pl.BlockSpec(memory_space=pltpu.HBM)] * 6,
        out_specs=pl.BlockSpec(memory_space=pltpu.VMEM),
        scratch_shapes=[pltpu.SMEM((n,), jnp.int32)]
        + raw
        + [
            vmem(18, OWN),
            vmem(9, OWN),
            vmem(9, 4),
            vmem(9, 12),
            vmem(9, 12),
            vmem(11, PW),
            vmem(6, PW - 2),
            vmem(4, PW),
            vmem(3, 3),
            vmem(3, 3),
            vmem(3, 11),
            vmem(3, 11),
            vmem(3, OW),
            vmem(9, OW),
            vmem(9, SW),
            vmem(9, 2),
            vmem(9, 2),
            vmem(9, 10),
            vmem(9, 10),
            vmem(2, 3, SW + 2),
            vmem(3, SW),
            vmem(3, 2),
            vmem(3, 2),
            vmem(3, 10),
            vmem(3, 10),
            vmem(3, 20),
            pltpu.SemaphoreType.DMA((12,)),
            pltpu.SemaphoreType.DMA((12,)),
            pltpu.SemaphoreType.DMA((6,)),
        ],
        compiler_params=pltpu.CompilerParams(
            collective_id=0, has_side_effects=True, vmem_limit_bytes=64 * 1024 * 1024
        ),
    )(counts, resid, accum, mobility, trans, decouple)
    return value.reshape(3, CAP, 1024)


def solution(mesh):
    spec = P(None, ("groups", "gx"), None)
    return jax.shard_map(
        on_device,
        mesh=mesh,
        in_specs=(P("groups"),) + (spec,) * 5,
        out_specs=spec,
        check_vma=False,
    )
```

time: 24.5 us -> 17 us (0.69)
  the two profiles are of different devices: /device:TPU:11 before, /device:TPU:5 now
where the time goes in v4:
time: 17 us; the launch traced here: 16.8 us
  Pallas kernels  15.1 us (89%)
  local copies, waits for them, and re-layouts  1.64 us (10%)
    pallas_call x1, Pallas kernels, on_device(): pl.pallas_call(functools.partial(kernel, n), out_shape=jax.ShapeDtypeStru...  15.1 us
    reshape x1, local copies, waits for them, and re-layouts, on_device(): return value.reshape(3, CAP, 1024)  1.64 us

profile of v4, /device:TPU:5, one launch (start us, length us, event | category | flops | bytes accessed | tf_op | source)
XLA Modules:
  0.0 16.8 jit_solution(2124724867414640456)
XLA Ops:
  0.0 15.1 %shard_map.64 = f32[3,16,8,128]{3,2,1,0:T(8,128)} custom-call(s32[16]{0:T(128)} %counts_hbm.1, f32[3,16,1024]{2,1,0:T(8,128)} %resid_hbm.1, f32[9,16,1024]{2,1,0:T(8,128)} %accum_hbm.1, f32[9,16,1024]{2,1,0:T(8,128)} %mobility_hbm.1, f32[3,16,1024]{2,1,0:T(8,128)} %trans_hbm.1, f32[2,16,1024]{2,1,0:T(8,128)} %decouple_hbm.1), custom_call_target="tpu_custom_call" | custom-call | tf_op jit(solution)/shard_map/pallas_call | solution.py:426
  15.2 1.6 %reshape.3 = f32[3,16,1024]{2,1,0:T(8,128)} reshape(f32[3,16,8,128]{3,2,1,0:T(8,128)} %shard_map.64) | data formatting | bytes 393216 | tf_op jit(solution)/shard_map/reshape | solution.py:468

commit v5 on v4

v5 whole, which is shorter than its diff:
```python
import functools

import jax
import jax.numpy as jnp
from jax import lax
from jax.experimental import pallas as pl
from jax.experimental.pallas import tpu as pltpu
from jax.sharding import PartitionSpec as P

CX = 8
NZ = 32
CHEB = 6
SWEEPS = 6
CAP = 16
CHEB_LOW = 0.1
CHEB_HIGH = 2.0

LEAD = 9
OWN = LEAD + CAP + 1
PW = 22
SW = 16
OW = 12


def y_next(x, lane):
    r = pltpu.roll(x, 96, x.ndim - 1)
    return jnp.where(lane < 96, r, pltpu.roll(r, 7, x.ndim - 2))


def y_prev(x, lane):
    r = pltpu.roll(x, 32, x.ndim - 1)
    return jnp.where(lane >= 32, r, pltpu.roll(r, 1, x.ndim - 2))


def z_next(x):
    return pltpu.roll(x, 127, x.ndim - 1)


def z_prev(x):
    return pltpu.roll(x, 1, x.ndim - 1)


def kernel(
    n,
    counts_hbm,
    resid_hbm,
    accum_hbm,
    mobility_hbm,
    trans_hbm,
    decouple_hbm,
    out,
    counts,
    resid,
    accum,
    mobility,
    trans,
    decouple,
    own,
    pslot,
    pup,
    pbelow,
    pabove,
    qbelow,
    qabove,
    mbelow,
    mabove,
    pw,
    coef,
    state,
    bup,
    bdown,
    bbelow,
    babove,
    inverse,
    gain,
    gup,
    gdown,
    gbelow,
    gabove,
    carried,
    target,
    result,
    send_sem,
    recv_sem,
    load_sem,
):
    me = lax.axis_index("gx")
    pairs = [
        (counts_hbm, counts),
        (mobility_hbm, mobility),
        (accum_hbm, accum),
        (resid_hbm, resid),
        (trans_hbm, trans),
        (decouple_hbm, decouple),
    ]
    loads = [
        pltpu.make_async_copy(src, dst, load_sem.at[i]) for i, (src, dst) in enumerate(pairs)
    ]
    for load in loads:
        load.start()
    barrier = pltpu.get_barrier_semaphore()
    here = {-2: me > 1, -1: me > 0, 1: me < n - 1, 2: me < n - 2}
    for step in here:

        @pl.when(here[step])
        def _():
            pl.semaphore_signal(
                barrier, inc=1, device_id={"gx": me + step}, device_id_type=pl.DeviceIdType.MESH
            )

    loads[0].wait()
    start = jnp.int32(0)
    for part in range(n):
        start = start + jnp.where(part < me, counts[part], 0)
    count = counts[me]
    end = start + count
    count_low = counts[jnp.maximum(me - 1, 0)]
    count_high = counts[jnp.minimum(me + 1, n - 1)]
    base = CX * me
    drift = jnp.clip(start - base, -2, 2)
    drift_end = jnp.clip(end - base - CX, -2, 2)
    tail = jnp.clip(count, 4, 12)
    low_at = 2 - drift
    high_at = 2 - drift_end

    shape = (1, 8, 128)
    lane = lax.broadcasted_iota(jnp.int32, shape, 2)
    row = lax.broadcasted_iota(jnp.int32, shape, 1)
    keep_row = jnp.where((row < 7) | (lane < 96), 1.0, 0.0)
    keep_lane = jnp.where(lane % NZ < NZ - 1, 1.0, 0.0)

    def planes(first, length):
        return first + lax.broadcasted_iota(jnp.int32, (length, 8, 128), 0)

    def tiles(value):
        return value.reshape(CAP, 8, 128)

    blank = jnp.zeros((LEAD, 8, 128), jnp.float32)
    zero = jnp.zeros((1, 8, 128), jnp.float32)
    slot_ids = planes(0, CAP)
    held = slot_ids < count

    for load in loads[1:]:
        load.wait()
    one, two = decouple[0], decouple[1]
    fields = [
        tiles(mobility[0] + one * mobility[3] + two * mobility[6]),
        jnp.where(slot_ids + start < CX * n - 1, tiles(trans[0]), 0.0),
        tiles(resid[0] + one * resid[1] + two * resid[2]),
        tiles(accum[0] + one * accum[3] + two * accum[6]),
        tiles(trans[1]) * keep_row,
        tiles(trans[2]) * keep_lane,
        tiles(mobility[0]),
        tiles(mobility[3]),
        tiles(mobility[6]),
        tiles(accum[0]),
        tiles(accum[3]),
        tiles(accum[6]),
        tiles(resid[0]),
        tiles(resid[1]),
        tiles(resid[2]),
    ]
    for i, value in enumerate(fields):
        pslot[i, :LEAD] = blank
        pslot[i, LEAD : LEAD + CAP] = jnp.where(held, value, 0.0)
        pslot[i, LEAD + CAP :] = zero
    for i in range(15):
        pup[i] = pslot[i, pl.ds(LEAD + tail - 5, 5)]

    known = jnp.int32(0)
    for step in here:
        known = known + here[step].astype(jnp.int32)
    pl.semaphore_wait(barrier, known)

    def send(src, dst, step, slot):
        return pltpu.make_async_remote_copy(
            src_ref=src,
            dst_ref=dst,
            send_sem=send_sem.at[slot],
            recv_sem=recv_sem.at[slot],
            device_id={"gx": me + step},
            device_id_type=pl.DeviceIdType.MESH,
        )

    L = LEAD
    phase_a = [
        (1, send(pup.at[0:2], pbelow.at[0:2, 4:9], 1, 0)),
        (-1, send(pslot.at[0:2, L : L + 5], pabove.at[0:2, 4:9], -1, 1)),
        (1, send(pup.at[2:6, 1:5], pbelow.at[2:6, 5:9], 1, 2)),
        (-1, send(pslot.at[2:6, L : L + 4], pabove.at[2:6, 4:8], -1, 3)),
        (2, send(pup.at[0:2, 4:5], qbelow, 2, 4)),
        (-2, send(pslot.at[0:2, L : L + 1], qabove, -2, 5)),
    ]
    phase_m = [
        (1, send(pup.at[6:9, 2:5], mbelow.at[0:3, 6:9], 1, 6)),
        (-1, send(pslot.at[6:9, L : L + 3], mabove.at[0:3, 4:7], -1, 7)),
        (1, send(pup.at[9:15, 3:5], mbelow.at[3:9, 7:9], 1, 8)),
        (-1, send(pslot.at[9:15, L : L + 2], mabove.at[3:9, 4:6], -1, 9)),
    ]
    phase_b = [
        (1, send(bup, bbelow.at[:, 4:9], 1, 10)),
        (-1, send(bdown, babove.at[:, 4:9], -1, 11)),
    ]
    phase_g = [
        (1, send(gup, gbelow.at[:, 4:6], 1, 12)),
        (-1, send(gdown, gabove.at[:, 4:6], -1, 13)),
    ]

    def begin(phase):
        for step, copy in phase:

            @pl.when(here[step])
            def _(copy=copy):
                copy.start()

    def arrive(phase):
        for step, copy in phase:

            @pl.when(here[-step])
            def _(copy=copy):
                copy.wait_recv()

    begin(phase_a)
    begin(phase_m)

    rest = [(mobility, 3 * i + c) for i in range(3) for c in (1, 2)]
    rest += [(accum, 3 * i + c) for i in range(3) for c in (1, 2)]
    for i, (ref, at) in enumerate(rest):
        own[i, :LEAD] = blank
        own[i, LEAD : LEAD + CAP] = tiles(ref[at])
        own[i, LEAD + CAP :] = zero

    arrive(phase_a)

    spot_low, spot_high = planes(base - 7, 9), planes(base + 6, 9)

    def near_low(width):
        return (spot_low >= start - width) & (spot_low < start) & (spot_low >= 0)

    def near_high(width):
        return (spot_high >= end) & (spot_high < end + width) & (spot_high < CX * n)

    def assemble(i):
        width = 5 if i < 2 else 4 if i < 6 else 3 if i < 9 else 2
        mine = pslot[i, pl.ds(low_at, PW)]
        below, above, at = (pbelow, pabove, i) if i < 6 else (mbelow, mabove, i - 6)
        low = jnp.where(near_low(width), below[at, pl.ds(low_at, 9)], mine[0:9])
        high = jnp.where(near_high(width), above[at, pl.ds(high_at, 9)], mine[13:22])
        if i < 2:
            beyond = (spot_low == start - 5) & (count_low == 4) & (spot_low >= 0)
            low = jnp.where(beyond, qbelow[i], low)
            beyond = (spot_high == end + 4) & (count_high == 4) & (spot_high < CX * n)
            high = jnp.where(beyond, qabove[i], high)
        pw[i, 0:9] = low
        pw[i, 9:13] = mine[9:13]
        pw[i, 13:22] = high

    for i in range(6):
        assemble(i)
    inner = slice(1, PW - 1)
    pw[15, inner] = y_prev(pw[4, inner], lane)
    pw[16, inner] = z_prev(pw[5, inner])

    def face_total(first, length):
        span = slice(first, first + length)
        total = pw[1, span] + pw[1, first - 1 : first - 1 + length]
        return total + pw[4, span] + pw[15, span] + pw[5, span] + pw[16, span]

    spot = planes(base - 2, OW)
    mine = (spot >= start) & (spot < end)
    faces = face_total(5, OW)

    def block(i):
        return own[i, pl.ds(low_at + 5, OW)]

    m = []
    for i in range(3):
        m += [pslot[6 + i, pl.ds(low_at + 5, OW)], block(2 * i), block(2 * i + 1)]
    a = []
    for i in range(3):
        a += [pslot[9 + i, pl.ds(low_at + 5, OW)], block(6 + 2 * i), block(7 + 2 * i)]
    b = [a[i] + faces * m[i] for i in range(9)]
    cofactor = [
        b[4] * b[8] - b[5] * b[7],
        b[2] * b[7] - b[1] * b[8],
        b[1] * b[5] - b[2] * b[4],
        b[5] * b[6] - b[3] * b[8],
        b[0] * b[8] - b[2] * b[6],
        b[2] * b[3] - b[0] * b[5],
        b[3] * b[7] - b[4] * b[6],
        b[1] * b[6] - b[0] * b[7],
        b[0] * b[4] - b[1] * b[3],
    ]
    det = b[0] * cofactor[0] + b[1] * cofactor[3] + b[2] * cofactor[6]
    scale = 1.0 / jnp.where(mine, det, 1.0)
    inv = [jnp.where(mine, value * scale, 0.0) for value in cofactor]
    edge = jnp.zeros((2, 8, 128), jnp.float32)
    for i in range(3):
        for c in range(3):
            inverse[3 * i + c] = inv[3 * i + c]
            value = m[3 * i] * inv[c] + m[3 * i + 1] * inv[3 + c] + m[3 * i + 2] * inv[6 + c]
            gain[3 * i + c, 0:2] = edge
            gain[3 * i + c, 2 : 2 + OW] = jnp.where(mine, value, 0.0)
            gain[3 * i + c, 2 + OW : SW] = edge
    for i in range(9):
        gup[i] = gain[i, pl.ds(10 + drift_end, 2)]
        gdown[i] = gain[i, pl.ds(4 + drift, 2)]
    begin(phase_g)

    middle = 0.5 * (CHEB_HIGH + CHEB_LOW)
    radius = 0.5 * (CHEB_HIGH - CHEB_LOW)
    aspect = middle / radius
    for i in range(2):
        state[i, 0:1] = zero
        state[i, PW - 1 : PW] = zero
    lam = pw[0]
    cx_all = pw[1, 0 : PW - 1] * (lam[0 : PW - 1] + lam[1:PW]) * 0.5
    cx, cx_down = cx_all[1:], cx_all[:-1]
    lam = lam[inner]
    cy = pw[4, inner] * (lam + y_next(lam, lane)) * 0.5
    cz = pw[5, inner] * (lam + z_next(lam)) * 0.5
    cy_down = y_prev(cy, lane)
    cz_down = z_prev(cz)
    pivot = pw[3, inner] + cx + cx_down + cy + cy_down + cz + cz_down
    spot = planes(base - 6, PW - 2)
    valid = (spot >= start - 4) & (spot < end + 4) & (spot >= 0) & (spot < CX * n)
    scale = 1.0 / jnp.where(valid, pivot, 1.0)
    for i, value in enumerate((cx, cx_down, cy, cy_down, cz, cz_down)):
        coef[i] = value * scale
    scaled = pw[2, inner] * scale
    state[2, inner] = scaled
    state[0, inner] = scaled / middle
    state[3, inner] = scaled / middle

    def advance(iteration, factor):
        now, later = iteration % 2, (iteration + 1) % 2
        factor_next = 1.0 / (2.0 * aspect - factor)
        d = state[now, inner]
        across = coef[0] * state[now, 2:PW] + coef[1] * state[now, 0 : PW - 2]
        across = across + coef[2] * y_next(d, lane) + coef[3] * y_prev(d, lane)
        across = across + coef[4] * z_next(d) + coef[5] * z_prev(d)
        e = state[2, inner] - d + across
        state[2, inner] = e
        d = (factor_next * factor) * d + (2.0 * factor_next / radius) * e
        state[later, inner] = d
        state[3, inner] = state[3, inner] + d
        return factor_next

    factor = 1.0 / aspect
    for iteration in range(3):
        factor = advance(iteration, factor)

    for i in range(3):
        bup[i] = state[1 + i, pl.ds(10 + drift_end, 5)]
        bdown[i] = state[1 + i, pl.ds(7 + drift, 5)]
    begin(phase_b)

    arrive(phase_m)
    for i in range(6, 15):
        assemble(i)
    span = slice(3, 3 + SW)
    faces = face_total(3, SW)
    columns = [pw[9 + i, span] + faces * pw[6 + i, span] for i in range(3)]

    arrive(phase_b)
    for i in range(3):
        low = jnp.where(near_low(5), bbelow[i, pl.ds(low_at, 9)], state[1 + i, 0:9])
        high = jnp.where(near_high(5), babove[i, pl.ds(high_at, 9)], state[1 + i, 13:22])
        state[1 + i, 0:9] = low
        state[1 + i, 13:22] = high
    for iteration in range(3, CHEB - 1):
        factor = advance(iteration, factor)

    for i in range(3):
        for slot in range(2):
            carried[slot, i, 0:1] = zero
            carried[slot, i, SW + 1 : SW + 2] = zero

    def across_of(first, u, up, down, length):
        here_planes = slice(first, first + length)
        value = pw[1, here_planes] * up + pw[1, first - 1 : first - 1 + length] * down
        value = value + pw[4, here_planes] * y_next(u, lane) + pw[15, here_planes] * y_prev(u, lane)
        return value + pw[5, here_planes] * z_next(u) + pw[16, here_planes] * z_prev(u)

    spot = planes(base - 4, SW)
    inside = (spot >= start - 2) & (spot < end + 2) & (spot >= 0) & (spot < CX * n)
    pressure = state[3, 2 : 4 + SW]
    for i in range(3):
        v = pw[6 + i, 2 : 4 + SW] * pressure
        sums = across_of(3, v[1 : 1 + SW], v[2 : 2 + SW], v[0:SW], SW)
        goal = pw[12 + i, span] - columns[i] * pressure[1 : 1 + SW] + sums
        target[i] = jnp.where(inside, goal, 0.0)

    def merge(ref, i, below, above):
        low = jnp.where(near_low(2)[3:9], below[i, pl.ds(low_at, 6)], ref[i, 0:6])
        high = jnp.where(near_high(2)[0:6], above[i, pl.ds(high_at, 6)], ref[i, 10:16])
        ref[i, 0:6] = low
        ref[i, 10:16] = high

    arrive(phase_g)
    for i in range(9):
        merge(gain, i, gbelow, gabove)

    def times(blocks, vector):
        return [
            blocks[3 * i] * vector[0]
            + blocks[3 * i + 1] * vector[1]
            + blocks[3 * i + 2] * vector[2]
            for i in range(3)
        ]

    first = times(gain, [target[i] for i in range(3)])
    for i in range(3):
        carried[0, i, 1 : 1 + SW] = first[i]
    for sweep in range(SWEEPS - 2):
        now, later = sweep % 2, (sweep + 1) % 2
        vector = []
        for i in range(3):
            u = carried[now, i]
            sums = across_of(3, u[1 : 1 + SW], u[2 : 2 + SW], u[0:SW], SW)
            vector.append(target[i] + sums)
        new = times(gain, vector)
        for i in range(3):
            carried[later, i, 1 : 1 + SW] = new[i]
    now = (SWEEPS - 2) % 2
    vector = []
    for i in range(3):
        u = carried[now, i, 2 : 4 + OW]
        sums = across_of(5, u[1 : 1 + OW], u[2 : 2 + OW], u[0:OW], OW)
        vector.append(target[i, 2 : 2 + OW] + sums)
    new = times(inverse, vector)
    new[0] = new[0] + state[3, 5 : 5 + OW]
    for i in range(3):
        result[i, 0:OW] = new[i]
        value = result[i, pl.ds(2 + drift, CAP)]
        out[i] = jnp.where(held, value, 0.0)

    for step, copy in phase_a + phase_m + phase_b + phase_g:

        @pl.when(here[step])
        def _(copy=copy):
            copy.wait_send()


def on_device(counts, resid, accum, mobility, trans, decouple):
    n = lax.axis_size("gx")
    f32 = jnp.float32

    def vmem(*dims):
        return pltpu.VMEM(dims + (8, 128), f32)

    raw = [pltpu.VMEM((fields, CAP, 1024), f32) for fields in (3, 9, 9, 3, 2)]
    value = pl.pallas_call(
        functools.partial(kernel, n),
        out_shape=jax.ShapeDtypeStruct((3, CAP, 8, 128), f32),
        in_specs=[pl.BlockSpec(memory_space=pltpu.HBM)] * 6,
        out_specs=pl.BlockSpec(memory_space=pltpu.VMEM),
        scratch_shapes=[pltpu.SMEM((n,), jnp.int32)]
        + raw
        + [
            vmem(12, OWN),
            vmem(15, OWN),
            vmem(15, 5),
            vmem(6, 13),
            vmem(6, 13),
            vmem(2, 1),
            vmem(2, 1),
            vmem(9, 13),
            vmem(9, 13),
            vmem(17, PW),
            vmem(6, PW - 2),
            vmem(4, PW),
            vmem(3, 5),
            vmem(3, 5),
            vmem(3, 13),
            vmem(3, 13),
            vmem(9, OW),
            vmem(9, SW),
            vmem(9, 2),
            vmem(9, 2),
            vmem(9, 10),
            vmem(9, 10),
            vmem(2, 3, SW + 2),
            vmem(3, SW),
            vmem(3, 20),
            pltpu.SemaphoreType.DMA((14,)),
            pltpu.SemaphoreType.DMA((14,)),
            pltpu.SemaphoreType.DMA((6,)),
        ],
        compiler_params=pltpu.CompilerParams(
            collective_id=0, has_side_effects=True, vmem_limit_bytes=64 * 1024 * 1024
        ),
    )(counts, resid, accum, mobility, trans, decouple)
    return value.reshape(3, CAP, 1024)


def solution(mesh):
    spec = P(None, ("groups", "gx"), None)
    return jax.shard_map(
        on_device,
        mesh=mesh,
        in_specs=(P("groups"),) + (spec,) * 5,
        out_specs=spec,
        check_vma=False,
    )
```

time: 17 us -> 17.2 us (1.012)
  Pallas kernels: 15.1 us -> 15.4 us
    pallas_call x1, Pallas kernels: 15.1 us -> 15.4 us  [on_device(): pl.pallas_call(functools.partial(kernel, n), out_shape=jax.ShapeDtypeStru...]
where the time goes in v5:
time: 17.2 us; the launch traced here: 17 us
  Pallas kernels  15.4 us (90%)
  local copies, waits for them, and re-layouts  1.64 us (10%)
    pallas_call x1, Pallas kernels, on_device(): pl.pallas_call(functools.partial(kernel, n), out_shape=jax.ShapeDtypeStru...  15.4 us
    reshape x1, local copies, waits for them, and re-layouts, on_device(): return value.reshape(3, CAP, 1024)  1.64 us

profile of v5, /device:TPU:5, one launch (start us, length us, event | category | flops | bytes accessed | tf_op | source)
XLA Modules:
  0.0 17.0 jit_solution(1351994605530912377)
XLA Ops:
  0.0 15.4 %shard_map.64 = f32[3,16,8,128]{3,2,1,0:T(8,128)} custom-call(s32[16]{0:T(128)} %counts_hbm.1, f32[3,16,1024]{2,1,0:T(8,128)} %resid_hbm.1, f32[9,16,1024]{2,1,0:T(8,128)} %accum_hbm.1, f32[9,16,1024]{2,1,0:T(8,128)} %mobility_hbm.1, f32[3,16,1024]{2,1,0:T(8,128)} %trans_hbm.1, f32[2,16,1024]{2,1,0:T(8,128)} %decouple_hbm.1), custom_call_target="tpu_custom_call" | custom-call | tf_op jit(solution)/shard_map/pallas_call | solution.py:453
  15.4 1.6 %reshape.3 = f32[3,16,1024]{2,1,0:T(8,128)} reshape(f32[3,16,8,128]{3,2,1,0:T(8,128)} %shard_map.64) | data formatting | bytes 393216 | tf_op jit(solution)/shard_map/reshape | solution.py:494

commit v6 on v4

--- a/solution.py
+++ b/solution.py
@@ -60,6 +60,8 @@
     pup,
     pbelow,
     pabove,
+    mbelow,
+    mabove,
     pw,
     coef,
     state,
@@ -179,8 +181,8 @@
         (-1, send(pslot.at[2:6, L : L + 3], pabove.at[2:6, 4:7], -1, 3)),
     ]
     phase_m = [
-        (1, send(pup.at[6:9, 3:4], pbelow.at[6:9, 7:8], 1, 4)),
-        (-1, send(pslot.at[6:9, L : L + 1], pabove.at[6:9, 4:5], -1, 5)),
+        (1, send(pup.at[6:9, 3:4], mbelow.at[:, 7:8], 1, 4)),
+        (-1, send(pslot.at[6:9, L : L + 1], mabove.at[:, 4:5], -1, 5)),
     ]
     phase_b = [
         (1, send(bup, bbelow.at[:, 4:7], 1, 6)),
@@ -210,7 +212,6 @@
                 copy.wait_recv()
 
     begin(phase_a)
-    begin(phase_m)
 
     rest = [(mobility, 3 * i + c) for i in range(3) for c in (1, 2)]
     rest += [(accum, i) for i in range(9)] + [(resid, i) for i in range(3)]
@@ -219,7 +220,6 @@
         own[i, LEAD:] = tiles(ref[at])
 
     arrive(phase_a)
-    arrive(phase_m)
 
     spot_low, spot_high = planes(base - 6, 8), planes(base + 6, 8)
 
@@ -229,12 +229,16 @@
     def near_high(width):
         return (spot_high >= end) & (spot_high < end + width) & (spot_high < CX * n)
 
-    for i in range(9):
+    def assemble(i):
         width = 4 if i < 2 else 3 if i < 6 else 1
+        below, above, at = (pbelow, pabove, i) if i < 6 else (mbelow, mabove, i - 6)
         mine = pslot[i, pl.ds(low_at, PW)]
-        pw[i, 0:8] = jnp.where(near_low(width), pbelow[i, pl.ds(low_at, 8)], mine[0:8])
+        pw[i, 0:8] = jnp.where(near_low(width), below[at, pl.ds(low_at, 8)], mine[0:8])
         pw[i, 8:12] = mine[8:12]
-        pw[i, 12:20] = jnp.where(near_high(width), pabove[i, pl.ds(high_at, 8)], mine[12:20])
+        pw[i, 12:20] = jnp.where(near_high(width), above[at, pl.ds(high_at, 8)], mine[12:20])
+
+    for i in range(6):
+        assemble(i)
 
     middle = 0.5 * (CHEB_HIGH + CHEB_LOW)
     radius = 0.5 * (CHEB_HIGH - CHEB_LOW)
@@ -286,6 +290,7 @@
         bup[i] = state[1 + i, pl.ds(11 + drift_end, 3)]
         bdown[i] = state[1 + i, pl.ds(6 + drift, 3)]
     begin(phase_b)
+    begin(phase_m)
 
     spot = planes(base - 2, OW)
     mine = (spot >= start) & (spot < end)
@@ -298,7 +303,7 @@
 
     m = []
     for i in range(3):
-        m += [pw[6 + i, middle_planes], block(2 * i), block(2 * i + 1)]
+        m += [pslot[6 + i, pl.ds(low_at + 4, OW)], block(2 * i), block(2 * i + 1)]
     b = [block(6 + i) + faces * m[i] for i in range(9)]
     cofactor = [
         b[4] * b[8] - b[5] * b[7],
@@ -336,6 +341,10 @@
         state[1 + i, 12:19] = high
     for iteration in range(3, CHEB - 1):
         factor = advance(iteration, factor)
+
+    arrive(phase_m)
+    for i in range(6, 9):
+        assemble(i)
 
     for i in range(3):
         for slot in range(2):
@@ -434,8 +443,10 @@
             vmem(18, OWN),
             vmem(9, OWN),
             vmem(9, 4),
-            vmem(9, 12),
-            vmem(9, 12),
+            vmem(6, 12),
+            vmem(6, 12),
+            vmem(3, 12),
+            vmem(3, 12),
             vmem(11, PW),
             vmem(6, PW - 2),
             vmem(4, PW),

time: 17 us -> 16.8 us (0.988)
  no operation moved by 1% of the time
where the time goes in v6:
time: 16.8 us; the launch traced here: 16.7 us
  Pallas kernels  15 us (89%)
  local copies, waits for them, and re-layouts  1.64 us (10%)
    pallas_call x1, Pallas kernels, on_device(): pl.pallas_call(functools.partial(kernel, n), out_shape=jax.ShapeDtypeStru...  15 us
    reshape x1, local copies, waits for them, and re-layouts, on_device(): return value.reshape(3, CAP, 1024)  1.64 us

profile of v6, /device:TPU:5, one launch (start us, length us, event | category | flops | bytes accessed | tf_op | source)
XLA Modules:
  0.0 16.7 jit_solution(907064869778719568)
XLA Ops:
  0.0 15.0 %shard_map.64 = f32[3,16,8,128]{3,2,1,0:T(8,128)} custom-call(s32[16]{0:T(128)} %counts_hbm.1, f32[3,16,1024]{2,1,0:T(8,128)} %resid_hbm.1, f32[9,16,1024]{2,1,0:T(8,128)} %accum_hbm.1, f32[9,16,1024]{2,1,0:T(8,128)} %mobility_hbm.1, f32[3,16,1024]{2,1,0:T(8,128)} %trans_hbm.1, f32[2,16,1024]{2,1,0:T(8,128)} %decouple_hbm.1), custom_call_target="tpu_custom_call" | custom-call | tf_op jit(solution)/shard_map/pallas_call | solution.py:435
  15.0 1.6 %reshape.3 = f32[3,16,1024]{2,1,0:T(8,128)} reshape(f32[3,16,8,128]{3,2,1,0:T(8,128)} %shard_map.64) | data formatting | bytes 393216 | tf_op jit(solution)/shard_map/reshape | solution.py:479
